TPU v7x, 32 devices: a whole 2x2x4 slice. The times are simulated.
32 devices in a mesh: cols: 16 (over z, x, core), spec: 2 (over y).
Axes of the slice: x: 2, y: 2, z: 4, core: 2. Of those that a mesh axis runs over, the one named last changes fastest.
Arguments:
- air_state: float32 [8, 256, 64, 128], P(None, 'cols', 'spec'), may hold values from -13 to 13, as said below
- courant_x: float32 [128], replicated, may hold values from -0.45 to 0.45
- courant_y: float32 [128], replicated, may hold values from -0.45 to 0.45
- cos_zenith: float32 [256, 64], P('cols', 'spec'), may hold values from 0.15 to 1
- sun_index: int32 [16, 2, 96], P('cols', 'spec'), may hold values from 0 to 511, as said below
- sun_count: int32 [2, 16], replicated, may hold values from 1 to 96, 384 in all within a row
- in_weight: bfloat16 [7, 128], replicated, may hold values from -3 to 3
- in_bias: float32 [128], replicated, may hold values from -4 to 4
- mid_weight: bfloat16 [128, 128], replicated, may hold values from -0.099609375 to 0.099609375
- mid_bias: float32 [128], replicated, may hold values from -2 to 2
- out_weight: bfloat16 [128, 256, 128], P(None, 'spec'), may hold values from -0.5 to 0.5
- out_bias: float32 [256], P('spec'), may hold values from -3 to 3
- absorption: float32 [256], P('spec'), may hold values from 0.00390625 to 0.0625
- solar_flux: float32 [256], P('spec'), may hold values from 0.03 to 1
Outputs:
- new_state: float32 [8, 256, 64, 128], P(None, 'cols', 'spec')
- solar_heating: float32 [256, 64, 128], P('cols', 'spec')
Inputs may be any that keep to these rules, and one draw needn't show every extreme that they name: For each tile (c, s) the entries sun_index[c, s, :] are distinct cell numbers m of that tile, naming the grid column (c * 16 + m // 32, s * 32 + m % 32); only the first sun_count[s, c] of them are sunlit, the others are unused. `sun_count`: entry [s, c] is the number of sunlit columns of tile (c, s); every row sums to exactly 384, and one entry of each row equals 96. `air_state`: the fields' values.
All inputs are finite; a program needn't handle non-finite values.
Results may differ from a plain program's by a relative error of at most 0.0023.
Values may be sent and summed in bfloat16 or wider, within the bound.
A program may use at most 64 MiB of HBM per device.

v0:
```python
import functools
import math

import jax
import jax.numpy as jnp
from jax import lax
from jax.sharding import PartitionSpec as P

NIN = 7
SECTIONS = 4


DIFFUSION = 0.05
ALBEDO = 0.3
DIFFUSIVITY = 1.66


def padded_2(cells, sides, width):
    for axis, dim in sides:
        count = lax.axis_size(axis)
        head = lax.slice_in_dim(cells, 0, width, axis=dim)
        tail = lax.slice_in_dim(cells, cells.shape[dim] - width, cells.shape[dim], axis=dim)
        cells = jnp.concatenate(
            [
                lax.ppermute(tail, axis, [(i, (i + 1) % count) for i in range(count)]),
                cells,
                lax.ppermute(head, axis, [((i + 1) % count, i) for i in range(count)]),
            ],
            axis=dim,
        )
    return cells


def section_update(padded, courant_x, courant_y):
    centre = padded[:, 1:-1, 1:-1]
    eastern = padded[:, 2:, 1:-1]
    western = padded[:, :-2, 1:-1]
    northern = padded[:, 1:-1, 2:]
    southern = padded[:, 1:-1, :-2]
    return (
        centre
        - 0.5 * courant_x * (eastern - western)
        + (0.5 * courant_x * courant_x + DIFFUSION) * (eastern - 2.0 * centre + western)
        - 0.5 * courant_y * (northern - southern)
        + (0.5 * courant_y * courant_y + DIFFUSION) * (northern - 2.0 * centre + southern)
    )


def radiate_block(features, slant_cos, weights):
    (
        in_weight,
        in_bias,
        mid_weight,
        mid_bias,
        out_weight,
        out_bias,
        absorption,
        solar_flux,
        lower_ones,
    ) = weights
    inputs = jnp.transpose(features, (2, 0, 1))
    first_sum = jnp.einsum("lni,ih->lnh", inputs, in_weight, preferred_element_type=jnp.float32)
    hidden_one = jax.nn.silu(first_sum + in_bias).astype(jnp.bfloat16)
    second = jnp.einsum("lnh,hk->lnk", hidden_one, mid_weight, preferred_element_type=jnp.float32)
    hidden_two = jax.nn.silu(second + mid_bias).astype(jnp.bfloat16)
    logits = jnp.einsum("lgh,lnh->lgn", out_weight, hidden_two, preferred_element_type=jnp.float32)
    depth_layer = absorption[:, None] * jax.nn.softplus(logits + out_bias[:, None])
    levels = depth_layer.shape[0]
    optical_depth = jnp.dot(
        lower_ones,
        depth_layer.reshape(levels, -1),
        precision=lax.Precision.HIGHEST,
        preferred_element_type=jnp.float32,
    ).reshape(depth_layer.shape)
    cosine = slant_cos.astype(jnp.float32)[None, None, :]
    column_total = optical_depth[-1:]
    source = solar_flux[None, :, None] * cosine
    down_top = source * jnp.exp(-(optical_depth - depth_layer) / cosine)
    down_bottom = source * jnp.exp(-optical_depth / cosine)
    up_base = ALBEDO * source * jnp.exp(-column_total / cosine)
    up_top = up_base * jnp.exp(-DIFFUSIVITY * (column_total - optical_depth + depth_layer))
    up_bottom = up_base * jnp.exp(-DIFFUSIVITY * (column_total - optical_depth))
    absorbed = down_top - down_bottom + up_bottom - up_top
    return jnp.transpose(jnp.sum(absorbed, axis=1))


def column_heating(pieces, first_row, weights):
    features, slant_cos = pieces
    rows_total = features.shape[0]
    block_rows = math.gcd(rows_total, 128)
    count_blocks = rows_total // block_rows
    shaped = (
        features.reshape(count_blocks, block_rows, features.shape[1], features.shape[2]),
        slant_cos.reshape(count_blocks, block_rows),
    )

    def one_block(block_pair):
        return radiate_block(block_pair[0], block_pair[1], weights)

    heated = lax.map(one_block, shaped)
    return heated.reshape(rows_total, features.shape[2])


def on_device(
    air_state,
    courant_x,
    courant_y,
    cos_zenith,
    sun_index,
    sun_count,
    in_weight,
    in_bias,
    mid_weight,
    mid_bias,
    out_weight,
    out_bias,
    absorption,
    solar_flux,
):
    fields, width_x, width_y, levels = air_state.shape
    current = air_state
    for section_number in range(SECTIONS):
        padded = padded_2(current, (("cols", 1), ("spec", 2)), 1)
        current = section_update(padded, courant_x, courant_y)
    level_index = jnp.arange(levels)
    lower_ones = (level_index[:, None] >= level_index[None, :]).astype(jnp.float32)
    weights = (
        in_weight,
        in_bias,
        mid_weight,
        mid_bias,
        out_weight,
        out_bias,
        absorption,
        solar_flux,
        lower_ones,
    )
    heating_fn = functools.partial(column_heating, weights=weights)
    cell_list = sun_index.reshape(-1)
    capacity = cell_list.shape[0]
    flat_state = air_state.reshape(fields, width_x * width_y, levels)
    features = jnp.transpose(jnp.take(flat_state[:NIN], cell_list, axis=1), (1, 0, 2)).astype(
        jnp.bfloat16
    )
    slant_cos = jnp.take(cos_zenith.reshape(-1), cell_list).astype(jnp.bfloat16)
    col_index = lax.axis_index("cols")
    spec_index = lax.axis_index("spec")
    own_row = sun_count[spec_index]
    own_count = own_row[col_index]
    positions = jnp.arange(capacity, dtype=jnp.int32)
    sunlit = positions < own_count
    tiles_x = own_row.shape[0]
    share_size = capacity // 4
    row_ends = jnp.cumsum(own_row)
    offset = row_ends[col_index] - own_count
    target = (
        jnp.arange(tiles_x, dtype=jnp.int32)[:, None] * share_size
        + jnp.arange(share_size, dtype=jnp.int32)[None, :]
        - offset
    )
    sending = (target >= 0) & (target < own_count)
    source_pos = jnp.clip(target, 0, capacity - 1)
    send_features = jnp.where(
        sending[:, :, None, None], features[source_pos], jnp.zeros((), jnp.bfloat16)
    )
    send_slant = jnp.where(sending, slant_cos[source_pos], jnp.zeros((), jnp.bfloat16))
    got_features, got_slant = (
        lax.all_to_all(send_features, "cols", split_axis=0, concat_axis=0, tiled=True),
        lax.all_to_all(send_slant, "cols", split_axis=0, concat_axis=0, tiled=True),
    )
    slot_index = jnp.arange(share_size, dtype=jnp.int32)
    slot_rank = col_index * share_size + slot_index
    anchor = jnp.searchsorted(row_ends, slot_rank, side="right")
    group_features = got_features[anchor, slot_index]
    group_slant = got_slant[anchor, slot_index]
    partial_terms = heating_fn(
        lax.all_gather((group_features, group_slant), "spec", axis=0, tiled=True), jnp.int32(0)
    )
    slot_heat = lax.psum_scatter(partial_terms, "spec", scatter_dimension=0, tiled=True)
    owner_match = jnp.arange(tiles_x, dtype=jnp.int32)[:, None] == anchor[None, :]
    send_back = jnp.where(owner_match[:, :, None], slot_heat[None, :, :], 0.0)
    returned = lax.all_to_all(send_back, "cols", split_axis=0, concat_axis=0, tiled=True)
    rank_mine = offset + positions
    holder = jnp.clip(rank_mine // share_size, 0, tiles_x - 1)
    heat_rows = returned[holder, rank_mine % share_size]
    heat_rows = jnp.where(sunlit[:, None], heat_rows, 0.0)
    heat_grid = jnp.zeros((width_x * width_y, levels), jnp.float32).at[cell_list].add(heat_rows)
    heat_grid = heat_grid.reshape(width_x, width_y, levels)
    new_state = current.at[0].add(heat_grid)
    return (new_state, heat_grid)


def solution(mesh):
    placed = (
        P(None, "cols", "spec", None),
        P(),
        P(),
        P("cols", "spec"),
        P("cols", "spec", None),
        P(),
        P(),
        P(),
        P(),
        P(),
        P(None, "spec", None),
        P("spec"),
        P("spec"),
        P("spec"),
    )
    return jax.shard_map(
        on_device,
        mesh=mesh,
        in_specs=placed,
        out_specs=(P(None, "cols", "spec", None), P("cols", "spec", None)),
        check_vma=False,
    )
```

profile of v0, /device:TPU:0, one launch (start us, length us, event | category | flops | bytes accessed | tf_op | source)
XLA Modules:
  0.0 182.0 jit_solution(8060775310949371219)
XLA Ops:
  7.2 3.2 %copy.65 = f32[8,16,32,128]{3,0,2,1:T(8,128)S(1)} copy(f32[8,16,32,128]{3,2,1,0:T(8,128)} %param.20) | data formatting | bytes 4194304 | tf_op args[0]
  12.9 5.0 %collective-permute-start = (f32[8,1,32,128]{3,0,2,1:T(8,128)S(1)}, f32[8,1,32,128]{3,0,2,1:T(8,128)S(1)}, u32[]{:S(2)}, u32[]{:S(2)}) collective-permute-start(f32[8,1,32,128]{3,0,2,1:T(8,128)S(1)} %get-tuple-element.277), channel_id=1, source_target_pairs={{2,0},{4,2},{6,4},{8,6},{10,8},{12,10},{14,12},{16,14},{18,16},{20... | collective-permute-start | bytes 393224 | tf_op jit(solution)/shard_map/ppermute | solution.py:27
  22.1 2.7 %gather_fusion.2 = bf16[384]{0:T(512)(128)(2,1)S(1)} fusion(bf16[96]{0:T(256)(128)(2,1)S(1)} %get-tuple-element.257, s32[1024]{0:T(1024)S(1)} %get-tuple-element.285), kind=kCustom, calls=%fused_computation.2 | custom fusion | bytes 3072 | tf_op jit(solution)/shard_map/gather | solution.py:166
  26.2 4.1 %all-to-all-start = ((bf16[16,1,24]{2,1,0:T(2,128)(2,1)}), bf16[16,1,24]{2,1,0:T(2,128)(2,1)}, u32[]{:S(2)}, u32[]{:S(2)}) async-start(bf16[16,1,24]{2,1,0:T(2,128)(2,1)} %copy.69), calls=%async_computation | async-start | bytes 16384 | tf_op jit(solution)/shard_map/all_to_all | solution.py:169
  34.1 3.8 %while.37 = (s32[]{:T(128)}, u32[24]{0:T(128)S(1)}, u32[24]{0:T(128)S(1)}, s32[16]{0:T(128)S(1)}, s32[]{:T(128)}, /*index=5*/s32[]{:T(128)}, s32[]{:T(128)}, s32[]{}) while((s32[]{:T(128)}, u32[24]{0:T(128)S(1)}, u32[24]{0:T(128)S(1)}, s32[16]{0:T(128)S(1)}, s32[]{:T(128)}, /*index=5*/s32[]{:T(128)}, s32[]{:T(128)}, s32[]{}) %tuple.78), condition=%wide.region_2.3_spmd.clone, body=%wide.region_1.2_spmd.clone.sunk | while | flops 1364 | bytes 5360 | solution.py:173
  40.5 2.1 %collective-permute-start.2 = (f32[8,18,1,128]{3,0,2,1:T(8,128)S(1)}, f32[8,18,1,128]{3,0,2,1:T(8,128)}, u32[]{:S(2)}, u32[]{:S(2)}) collective-permute-start(f32[8,18,1,128]{3,0,2,1:T(8,128)S(1)} %get-tuple-element.270), channel_id=1, source_target_pairs={{1,0},{0,1},{3,2},{2,3},{5,4},{4,5},{7,6},{6,7},{9,8},{8,9},{11,10... | collective-permute-start | bytes 221192 | tf_op jit(solution)/shard_map/ppermute | solution.py:27
  47.1 3.6 %multiply_add_fusion.3 = f32[8,16,32,128]{3,0,2,1:T(8,128)S(1)} fusion(f32[8,18,1,128]{3,0,2,1:T(8,128)} %collective-permute-done.2, f32[8,18,32,128]{3,0,2,1:T(8,128)} %copy-done.5, f32[8,18,1,128]{3,0,2,1:T(8,128)} %collective-permute-done.3, f32[8,16,32,128]{3,0,2,1:T(8,128)S(1)} %copy-done.4, f32[8,1,32,128]{3,0,2,1:T(8,128)S(1)} %collective-permute-done, ...), kind=kLoop, calls=%fused_computation.76 | loop fusion | flops 9961472 | bytes 6965248 | tf_op jit(solution)/shard_map/add | solution.py:41
  50.7 3.0 %collective-permute-start.4 = (f32[8,1,32,128]{3,0,2,1:T(8,128)S(1)}, f32[8,1,32,128]{3,0,2,1:T(8,128)S(1)}, u32[]{:S(2)}, u32[]{:S(2)}) collective-permute-start(f32[8,1,32,128]{3,0,2,1:T(8,128)S(1)} %get-tuple-element.276), channel_id=1, source_target_pairs={{2,0},{4,2},{6,4},{8,6},{10,8},{12,10},{14,12},{16,14},{18,16},{20... | collective-permute-start | bytes 393224 | tf_op jit(solution)/shard_map/ppermute | solution.py:27
  56.2 4.6 %collective-permute-done.5 = f32[8,1,32,128]{3,0,2,1:T(8,128)S(1)} collective-permute-done((f32[8,1,32,128]{3,0,2,1:T(8,128)S(1)}, f32[8,1,32,128]{3,0,2,1:T(8,128)S(1)}, u32[]{:S(2)}, u32[]{:S(2)}) %collective-permute-start.5) | collective-permute-done | bytes 131104 | tf_op jit(solution)/shard_map/ppermute | solution.py:25
  60.8 2.1 %collective-permute-start.6 = (f32[8,18,1,128]{3,0,2,1:T(8,128)S(1)}, f32[8,18,1,128]{3,0,2,1:T(8,128)S(1)}, u32[]{:S(2)}, u32[]{:S(2)}) collective-permute-start(f32[8,18,1,128]{3,0,2,1:T(8,128)S(1)} %get-tuple-element.268), channel_id=1, source_target_pairs={{1,0},{0,1},{3,2},{2,3},{5,4},{4,5},{7,6},{6,7},{9,8},{8,9},{11,10... | collective-permute-start | bytes 221192 | tf_op jit(solution)/shard_map/ppermute | solution.py:27
  69.2 5.4 %all-to-all-start.1 = ((bf16[16,24,7,128]{3,1,2,0:T(8,128)(2,1)}), bf16[16,24,7,128]{3,1,2,0:T(8,128)(2,1)S(1)}, u32[]{:S(2)}, u32[]{:S(2)}) async-start(bf16[16,24,7,128]{3,1,2,0:T(8,128)(2,1)} %copy_select_fusion), calls=%async_computation.1 | async-start | bytes 1376256 | tf_op jit(solution)/shard_map/all_to_all | solution.py:168
  81.6 4.9 %all-reduce = bf16[48]{0:T(256)(128)(2,1)S(1)} all-reduce(bf16[48]{0:T(256)(128)(2,1)S(1)} %dynamic-update-slice.3), channel_id=1, replica_groups=mesh['cols'=16,'spec'=2] {'spec'}, use_global_device_ids=true, to_apply=%add | all-reduce | flops 48 | bytes 192
  90.7 3.0 %collective-permute-start.12 = (f32[8,1,32,128]{3,0,2,1:T(8,128)}, f32[8,1,32,128]{3,0,2,1:T(8,128)S(1)}, u32[]{:S(2)}, u32[]{:S(2)}) collective-permute-start(f32[8,1,32,128]{3,0,2,1:T(8,128)} %get-tuple-element.272), channel_id=1, source_target_pairs={{2,0},{4,2},{6,4},{8,6},{10,8},{12,10},{14,12},{16,14},{18,16},{20... | collective-permute-start | bytes 393224 | tf_op jit(solution)/shard_map/ppermute | solution.py:27
  94.5 4.7 %all_gather.7 = bf16[48,7,128]{2,0,1:T(8,128)(2,1)S(1)} all-gather(bf16[24,7,128]{2,0,1:T(8,128)(2,1)S(1)} %copy.73), channel_id=1, replica_groups=mesh['cols'=16,'spec'=2] {'spec'}, dimensions={0}, use_global_device_ids=true | all-gather | bytes 129024 | tf_op jit(solution)/shard_map/all_gather | solution.py:177
  99.3 35.2 %while.36 = (s32[]{:T(128)}, f32[3,16,128]{2,1,0:T(8,128)S(1)}, f32[128]{0:T(128)}, bf16[3,16]{1,0:T(4,128)(2,1)}, f32[128]{0:T(128)S(1)}, /*index=5*/bf16[3,16,...) while((s32[]{:T(128)}, f32[3,16,128]{2,1,0:T(8,128)S(1)}, ...), condition=%wide.region_5.6_spmd.clone, body=%wide.region_3.5_spmd.clone.sunk | while | flops 550281216 | bytes 14942825 | solution.py:100
  100.8 4.5 %fusion.67 = f32[128,128,16]{1,2,0:T(8,128)S(1)} fusion(bf16[128,128,128]{2,1,0:T(8,128)(2,1)} %get-tuple-element.459, bf16[128,16,128]{2,0,1:T(8,128)(2,1)S(1)} %multiply_convert_fusion.3, f32[128]{0:T(128)S(1)} %get-tuple-element.460, f32[128]{0:T(128)S(1)} %get-tuple-element.453), kind=kOutput, calls=%fused_computation.23.clone.1 | convolution fusion | flops 69206016 | bytes 5768192 | tf_op jit(solution)/shard_map/while/body/eval_jaxpr/lgh,lnh->lgn/dot_general | solution.py:66
  112.6 4.5 %fusion.67 = f32[128,128,16]{1,2,0:T(8,128)S(1)} fusion(bf16[128,128,128]{2,1,0:T(8,128)(2,1)} %get-tuple-element.459, bf16[128,16,128]{2,0,1:T(8,128)(2,1)S(1)} %multiply_convert_fusion.3, f32[128]{0:T(128)S(1)} %get-tuple-element.460, f32[128]{0:T(128)S(1)} %get-tuple-element.453), kind=kOutput, calls=%fused_computation.23.clone.1 | convolution fusion | flops 69206016 | bytes 5768192 | tf_op jit(solution)/shard_map/while/body/eval_jaxpr/lgh,lnh->lgn/dot_general | solution.py:66
  124.3 4.5 %fusion.67 = f32[128,128,16]{1,2,0:T(8,128)S(1)} fusion(bf16[128,128,128]{2,1,0:T(8,128)(2,1)} %get-tuple-element.459, bf16[128,16,128]{2,0,1:T(8,128)(2,1)S(1)} %multiply_convert_fusion.3, f32[128]{0:T(128)S(1)} %get-tuple-element.460, f32[128]{0:T(128)S(1)} %get-tuple-element.453), kind=kOutput, calls=%fused_computation.23.clone.1 | convolution fusion | flops 69206016 | bytes 5768192 | tf_op jit(solution)/shard_map/while/body/eval_jaxpr/lgh,lnh->lgn/dot_general | solution.py:66
  138.1 6.3 %reduce-scatter.4.cloned.1.call-done = f32[24,128]{1,0:T(8,128)} async-done(((f32[48,128]{1,0:T(8,128)}), f32[24,128]{1,0:T(8,128)}) %reduce-scatter.4.cloned.1.call-update) | async-done | bytes 12304
  145.9 5.6 %all-to-all-start.2 = ((f32[16,24,128]{2,1,0:T(8,128)}), f32[16,24,128]{2,1,0:T(8,128)S(1)}, u32[]{:S(2)}, u32[]{:S(2)}) async-start(f32[16,24,128]{2,1,0:T(8,128)} %broadcast_select_fusion.2), calls=%async_computation.2 | async-start | bytes 393216 | tf_op jit(solution)/shard_map/all_to_all | solution.py:182
  151.5 2.4 %multiply_add_fusion = f32[8,16,32,128]{3,0,2,1:T(8,128)} fusion(f32[8,18,1,128]{3,0,2,1:T(8,128)S(1)} %collective-permute-done.14, f32[8,1,32,128]{3,0,2,1:T(8,128)S(1)} %collective-permute-done.12, f32[8,16,32,128]{3,0,2,1:T(8,128)S(1)} %copy-done.1, f32[8,1,32,128]{3,0,2,1:T(8,128)S(1)} %collective-permute-done.13, ...), kind=kLoop, calls=%fused_computation.73 | loop fusion | flops 12058624 | bytes 4605952 | tf_op jit(solution)/shard_map/add | solution.py:41
  153.9 6.5 %all-to-all-done.2 = f32[16,24,128]{2,1,0:T(8,128)S(1)} async-done(((f32[16,24,128]{2,1,0:T(8,128)}), f32[16,24,128]{2,1,0:T(8,128)S(1)}, u32[]{:S(2)}, u32[]{:S(2)}) %all-to-all-start.2) | async-done | bytes 196640 | tf_op jit(solution)/shard_map/all_to_all | solution.py:182
  164.2 7.7 %scatter-add.13 = f32[8,16,32,128]{3,0,2,1:T(8,128)} dynamic-update-slice(f32[8,16,32,128]{3,0,2,1:T(8,128)} %multiply_add_fusion, f32[1,16,32,128]{3,0,2,1:T(1,128)S(1)} %slice_add_fusion, s32[]{:T(128)} %constant.165.clone.1, s32[]{:T(128)} %constant.165.clone.1, s32[]{:T(128)} %constant.165.clone.1, s32[]{:T(128)} %constant.165.clone.1) | dynamic-update-slice | bytes 524292 | tf_op jit(solution)/shard_map/scatter-add | solution.py:189
  171.9 3.3 %copy.76 = f32[8,16,32,128]{3,2,1,0:T(8,128)} copy(f32[8,16,32,128]{3,0,2,1:T(8,128)} %scatter-add.13) | data formatting | bytes 4194304
  (207 shorter events, 71.5 us)
Async XLA Ops:
  12.4 26.3 %collective-permute-start.1 = (f32[8,1,32,128]{3,0,2,1:T(8,128)}, f32[8,1,32,128]{3,0,2,1:T(8,128)S(1)}, u32[]{:S(2)}, u32[]{:S(2)}) collective-permute-start(f32[8,1,32,128]{3,0,2,1:T(8,128)} %get-tuple-element.278), channel_id=1, source_target_pairs={{0,2},{2,4},{4,6},{6,8},{8,10},{10,12},{12,14},{14,16},{16,18},{18... | collective-permute-start | bytes 393224 | tf_op jit(solution)/shard_map/ppermute | solution.py:25
  12.9 27.5 %collective-permute-start = (f32[8,1,32,128]{3,0,2,1:T(8,128)S(1)}, f32[8,1,32,128]{3,0,2,1:T(8,128)S(1)}, u32[]{:S(2)}, u32[]{:S(2)}) collective-permute-start(f32[8,1,32,128]{3,0,2,1:T(8,128)S(1)} %get-tuple-element.277), channel_id=1, source_target_pairs={{2,0},{4,2},{6,4},{8,6},{10,8},{12,10},{14,12},{16,14},{18,16},{20... | collective-permute-start | bytes 393224 | tf_op jit(solution)/shard_map/ppermute | solution.py:27
  26.2 43.0 %all-to-all-start = ((bf16[16,1,24]{2,1,0:T(2,128)(2,1)}), bf16[16,1,24]{2,1,0:T(2,128)(2,1)}, u32[]{:S(2)}, u32[]{:S(2)}) async-start(bf16[16,1,24]{2,1,0:T(2,128)(2,1)} %copy.69), calls=%async_computation | async-start | bytes 16384 | tf_op jit(solution)/shard_map/all_to_all | solution.py:169
  40.5 4.9 %collective-permute-start.2 = (f32[8,18,1,128]{3,0,2,1:T(8,128)S(1)}, f32[8,18,1,128]{3,0,2,1:T(8,128)}, u32[]{:S(2)}, u32[]{:S(2)}) collective-permute-start(f32[8,18,1,128]{3,0,2,1:T(8,128)S(1)} %get-tuple-element.270), channel_id=1, source_target_pairs={{1,0},{0,1},{3,2},{2,3},{5,4},{4,5},{7,6},{6,7},{9,8},{8,9},{11,10... | collective-permute-start | bytes 221192 | tf_op jit(solution)/shard_map/ppermute | solution.py:27
  42.6 4.5 %collective-permute-start.3 = (f32[8,18,1,128]{3,0,2,1:T(8,128)S(1)}, f32[8,18,1,128]{3,0,2,1:T(8,128)}, u32[]{:S(2)}, u32[]{:S(2)}) collective-permute-start(f32[8,18,1,128]{3,0,2,1:T(8,128)S(1)} %get-tuple-element.269), channel_id=1, source_target_pairs={{0,1},{1,0},{2,3},{3,2},{4,5},{5,4},{6,7},{7,6},{8,9},{9,8},{10,11... | collective-permute-start | bytes 221192 | tf_op jit(solution)/shard_map/ppermute | solution.py:25
  50.7 5.5 %collective-permute-start.4 = (f32[8,1,32,128]{3,0,2,1:T(8,128)S(1)}, f32[8,1,32,128]{3,0,2,1:T(8,128)S(1)}, u32[]{:S(2)}, u32[]{:S(2)}) collective-permute-start(f32[8,1,32,128]{3,0,2,1:T(8,128)S(1)} %get-tuple-element.276), channel_id=1, source_target_pairs={{2,0},{4,2},{6,4},{8,6},{10,8},{12,10},{14,12},{16,14},{18,16},{20... | collective-permute-start | bytes 393224 | tf_op jit(solution)/shard_map/ppermute | solution.py:27
  53.7 7.1 %collective-permute-start.5 = (f32[8,1,32,128]{3,0,2,1:T(8,128)S(1)}, f32[8,1,32,128]{3,0,2,1:T(8,128)S(1)}, u32[]{:S(2)}, u32[]{:S(2)}) collective-permute-start(f32[8,1,32,128]{3,0,2,1:T(8,128)S(1)} %get-tuple-element.275), channel_id=1, source_target_pairs={{0,2},{2,4},{4,6},{6,8},{8,10},{10,12},{12,14},{14,16},{16,18},{18... | collective-permute-start | bytes 393224 | tf_op jit(solution)/shard_map/ppermute | solution.py:25
  60.8 4.4 %collective-permute-start.6 = (f32[8,18,1,128]{3,0,2,1:T(8,128)S(1)}, f32[8,18,1,128]{3,0,2,1:T(8,128)S(1)}, u32[]{:S(2)}, u32[]{:S(2)}) collective-permute-start(f32[8,18,1,128]{3,0,2,1:T(8,128)S(1)} %get-tuple-element.268), channel_id=1, source_target_pairs={{1,0},{0,1},{3,2},{2,3},{5,4},{4,5},{7,6},{6,7},{9,8},{8,9},{11,10... | collective-permute-start | bytes 221192 | tf_op jit(solution)/shard_map/ppermute | solution.py:27
  62.9 4.4 %collective-permute-start.7 = (f32[8,18,1,128]{3,0,2,1:T(8,128)S(1)}, f32[8,18,1,128]{3,0,2,1:T(8,128)S(1)}, u32[]{:S(2)}, u32[]{:S(2)}) collective-permute-start(f32[8,18,1,128]{3,0,2,1:T(8,128)S(1)} %get-tuple-element.267), channel_id=1, source_target_pairs={{0,1},{1,0},{2,3},{3,2},{4,5},{5,4},{6,7},{7,6},{8,9},{9,8},{10,11... | collective-permute-start | bytes 221192 | tf_op jit(solution)/shard_map/ppermute | solution.py:25
  68.7 7.9 %collective-permute-start.8 = (f32[8,1,32,128]{3,0,2,1:T(8,128)S(1)}, f32[8,1,32,128]{3,0,2,1:T(8,128)S(1)}, u32[]{:S(2)}, u32[]{:S(2)}) collective-permute-start(f32[8,1,32,128]{3,0,2,1:T(8,128)S(1)} %get-tuple-element.274), channel_id=1, source_target_pairs={{2,0},{4,2},{6,4},{8,6},{10,8},{12,10},{14,12},{16,14},{18,16},{20... | collective-permute-start | bytes 393224 | tf_op jit(solution)/shard_map/ppermute | solution.py:27
  68.7 7.8 %collective-permute-start.9 = (f32[8,1,32,128]{3,0,2,1:T(8,128)S(1)}, f32[8,1,32,128]{3,0,2,1:T(8,128)S(1)}, u32[]{:S(2)}, u32[]{:S(2)}) collective-permute-start(f32[8,1,32,128]{3,0,2,1:T(8,128)S(1)} %get-tuple-element.273), channel_id=1, source_target_pairs={{0,2},{2,4},{4,6},{6,8},{8,10},{10,12},{12,14},{14,16},{16,18},{18... | collective-permute-start | bytes 393224 | tf_op jit(solution)/shard_map/ppermute | solution.py:25
  69.2 24.4 %all-to-all-start.1 = ((bf16[16,24,7,128]{3,1,2,0:T(8,128)(2,1)}), bf16[16,24,7,128]{3,1,2,0:T(8,128)(2,1)S(1)}, u32[]{:S(2)}, u32[]{:S(2)}) async-start(bf16[16,24,7,128]{3,1,2,0:T(8,128)(2,1)} %copy_select_fusion), calls=%async_computation.1 | async-start | bytes 1376256 | tf_op jit(solution)/shard_map/all_to_all | solution.py:168
  74.6 69.7 %reduce-scatter.4.cloned.1.call-start = ((), (), s32[]{:S(2)}) async-start(), calls=%async_computation.4 | async-start | bytes 36864
  76.6 10.6 %collective-permute-start.10 = (f32[8,18,1,128]{3,0,2,1:T(8,128)S(1)}, f32[8,18,1,128]{3,0,2,1:T(8,128)S(1)}, u32[]{:S(2)}, u32[]{:S(2)}) collective-permute-start(f32[8,18,1,128]{3,0,2,1:T(8,128)S(1)} %get-tuple-element.266), channel_id=1, source_target_pairs={{1,0},{0,1},{3,2},{2,3},{5,4},{4,5},{7,6},{6,7},{9,8},{8,9},{11,10... | collective-permute-start | bytes 221192 | tf_op jit(solution)/shard_map/ppermute | solution.py:27
  77.4 9.8 %collective-permute-start.11 = (f32[8,18,1,128]{3,0,2,1:T(8,128)S(1)}, f32[8,18,1,128]{3,0,2,1:T(8,128)S(1)}, u32[]{:S(2)}, u32[]{:S(2)}) collective-permute-start(f32[8,18,1,128]{3,0,2,1:T(8,128)S(1)} %get-tuple-element.265), channel_id=1, source_target_pairs={{0,1},{1,0},{2,3},{3,2},{4,5},{5,4},{6,7},{7,6},{8,9},{9,8},{10,11... | collective-permute-start | bytes 221192 | tf_op jit(solution)/shard_map/ppermute | solution.py:25
  90.7 44.4 %collective-permute-start.12 = (f32[8,1,32,128]{3,0,2,1:T(8,128)}, f32[8,1,32,128]{3,0,2,1:T(8,128)S(1)}, u32[]{:S(2)}, u32[]{:S(2)}) collective-permute-start(f32[8,1,32,128]{3,0,2,1:T(8,128)} %get-tuple-element.272), channel_id=1, source_target_pairs={{2,0},{4,2},{6,4},{8,6},{10,8},{12,10},{14,12},{16,14},{18,16},{20... | collective-permute-start | bytes 393224 | tf_op jit(solution)/shard_map/ppermute | solution.py:27
  93.6 41.4 %collective-permute-start.13 = (f32[8,1,32,128]{3,0,2,1:T(8,128)}, f32[8,1,32,128]{3,0,2,1:T(8,128)S(1)}, u32[]{:S(2)}, u32[]{:S(2)}) collective-permute-start(f32[8,1,32,128]{3,0,2,1:T(8,128)} %get-tuple-element.271), channel_id=1, source_target_pairs={{0,2},{2,4},{4,6},{6,8},{8,10},{10,12},{12,14},{14,16},{16,18},{18... | collective-permute-start | bytes 393224 | tf_op jit(solution)/shard_map/ppermute | solution.py:25
  134.4 17.1 %copy-start.1 = (f32[8,16,32,128]{3,0,2,1:T(8,128)S(1)}, f32[8,16,32,128]{3,0,2,1:T(8,128)}, u32[]{:S(2)}) copy-start(f32[8,16,32,128]{3,0,2,1:T(8,128)} %copy-done) | copy-start | bytes 6291460
  134.4 17.1 %copy-start.11 = (f32[128]{0:T(128)S(1)}, f32[128]{0:T(128)}, u32[]{:S(2)}) copy-start(f32[128]{0:T(128)} %get-tuple-element.281) | copy-start | bytes 1540
  134.4 17.1 %copy-start.13 = (f32[128]{0:T(128)S(1)}, f32[128]{0:T(128)}, u32[]{:S(2)}) copy-start(f32[128]{0:T(128)} %get-tuple-element.282) | copy-start | bytes 1540
  134.5 17.1 %copy-start.15 = (f32[128]{0:T(128)S(1)}, f32[128]{0:T(128)}, u32[]{:S(2)}) copy-start(f32[128]{0:T(128)} %get-tuple-element.283) | copy-start | bytes 1540
  136.0 15.5 %collective-permute-start.14 = (f32[8,18,1,128]{3,0,2,1:T(8,128)S(1)}, f32[8,18,1,128]{3,0,2,1:T(8,128)S(1)}, u32[]{:S(2)}, u32[]{:S(2)}) collective-permute-start(f32[8,18,1,128]{3,0,2,1:T(8,128)S(1)} %get-tuple-element.264), channel_id=1, source_target_pairs={{1,0},{0,1},{3,2},{2,3},{5,4},{4,5},{7,6},{6,7},{9,8},{8,9},{11,10... | collective-permute-start | bytes 221192 | tf_op jit(solution)/shard_map/ppermute | solution.py:27
  136.9 14.6 %collective-permute-start.15 = (f32[8,18,1,128]{3,0,2,1:T(8,128)S(1)}, f32[8,18,1,128]{3,0,2,1:T(8,128)S(1)}, u32[]{:S(2)}, u32[]{:S(2)}) collective-permute-start(f32[8,18,1,128]{3,0,2,1:T(8,128)S(1)} %get-tuple-element.263), channel_id=1, source_target_pairs={{0,1},{1,0},{2,3},{3,2},{4,5},{5,4},{6,7},{7,6},{8,9},{9,8},{10,11... | collective-permute-start | bytes 221192 | tf_op jit(solution)/shard_map/ppermute | solution.py:25
  145.9 14.6 %all-to-all-start.2 = ((f32[16,24,128]{2,1,0:T(8,128)}), f32[16,24,128]{2,1,0:T(8,128)S(1)}, u32[]{:S(2)}, u32[]{:S(2)}) async-start(f32[16,24,128]{2,1,0:T(8,128)} %broadcast_select_fusion.2), calls=%async_computation.2 | async-start | bytes 393216 | tf_op jit(solution)/shard_map/all_to_all | solution.py:182
  (26 other events, 196.1 us)
Sparse Core Ops, SparseCore 0:
  135.2 9.1 reduce-scatter.3
where the time goes:
time: 183 us; the launch traced here: 182 us
  local copies, waits for them, and re-layouts  46.2 us (25%)
  starting transfers between devices  35.5 us (19%)
  other arithmetic  27.9 us (15%)
  waiting for transfers between devices  24.5 us (13%)
  matrix products  21.2 us (12%)
  between operations  16.6 us (9%)
  blocking collectives  9.62 us (5%)
    ppermute x8, starting transfers between devices, padded_2(): lax.ppermute(head, axis, [((i + 1) % count, i) for i in range(count)])  16.9 us
    dot_general x3, matrix products, radiate_block(): jnp.einsum('lgh,lnh->lgn', out_weight, hidden_two, preferred_element_type...  13.5 us
    unnamed x68, local copies, waits for them, and re-layouts  13 us
    add x4, other arithmetic, section_update(): centre - 0.5 * courant_x * (eastern - western)  8.75 us
    ppermute x8, waiting for transfers between devices, padded_2(): lax.ppermute(tail, axis, [(i, (i + 1) % count) for i in range(count)])  8.17 us
    scatter-add x1, local copies, waits for them, and re-layouts, on_device(): new_state = current.at[0].add(heat_grid)  7.71 us
    all_to_all x1, waiting for transfers between devices, on_device(): lax.all_to_all(send_back, 'cols', split_axis=0, concat_axis=0, tiled=True)  6.52 us
    unnamed x2, waiting for transfers between devices  6.28 us
  transfers between devices with their start and end apart: 20, of which 8 were waited for; matrix products, arithmetic and copies ran while one was open for 40% of the time, Pallas kernels for 0%

commit v1 on v0

v1 whole, which is shorter than its diff:
```python
import functools

import jax
import jax.numpy as jnp
from jax import lax
from jax.experimental import pallas as pl
from jax.experimental.pallas import tpu as pltpu
from jax.sharding import PartitionSpec as P

SECTIONS = 4
DIFFUSION = 0.05
ALBEDO = 0.3
DIFFUSIVITY = 1.66
MESH = pl.DeviceIdType.MESH
F32 = jnp.float32
BF16 = jnp.bfloat16
VMEM_LIMIT = 56 * 1024 * 1024


def cell_column(ranks, counts, index_row, spec, col):
    row = lax.broadcasted_iota(jnp.int32, counts.shape, 0)
    column = lax.broadcasted_iota(jnp.int32, counts.shape, 1)
    values = jnp.where(row == spec, counts, 0).astype(F32)
    offset = jnp.sum(jnp.where(column < col, values, 0.0), axis=(0, 1), keepdims=True)
    own = jnp.sum(jnp.where(column == col, values, 0.0), axis=(0, 1), keepdims=True)
    place = lax.broadcasted_iota(jnp.int32, (1, index_row.shape[1]), 1).astype(F32)
    table = jnp.where(place < own, index_row.astype(F32) + 1.0, 0.0)
    found = jnp.where(ranks - offset == place, table, 0.0)
    return jnp.sum(found, axis=1, keepdims=True) - 1.0


def rank_column(parity, half, share):
    within = lax.broadcasted_iota(jnp.int32, (share, 1), 0)
    return jnp.concatenate(
        [((2 * k + parity) * share + within).astype(F32) for k in range(half)], axis=0
    )


def pack_kernel(share, half, width_y, halo, place_ref, air_ref, cos_ref, index_ref, count_ref,
                send_ref, xlow_ref, xhigh_ref, ylow_ref, yhigh_ref, picked):
    fields, cells, levels = air_ref.shape[0], air_ref.shape[1], air_ref.shape[2]
    width_x = cells // width_y
    inputs = fields - 1
    col, spec = place_ref[0], place_ref[1]
    for parity in range(2):
        cell = cell_column(
            rank_column(parity, half, share), count_ref[...], index_ref[0], spec, col
        )
        slots = cell.shape[0]
        lane = lax.broadcasted_iota(jnp.int32, (slots, cells), 1).astype(F32)
        choose = jnp.where(cell == lane, 1.0, 0.0).astype(BF16)
        for i in range(inputs):
            picked[i] = jnp.dot(
                choose, air_ref[i].astype(BF16), preferred_element_type=F32
            )
        cell_x = jnp.floor((cell + 0.5) * (1.0 / width_y))
        cell_y = cell - cell_x * width_y
        lane_x = lax.broadcasted_iota(jnp.int32, (slots, width_x), 1).astype(F32)
        lane_y = lax.broadcasted_iota(jnp.int32, (slots, width_y), 1).astype(F32)
        by_x = jnp.dot(
            jnp.where(cell_x == lane_x, 1.0, 0.0).astype(BF16),
            cos_ref[...].astype(BF16),
            preferred_element_type=F32,
        )
        slant = jnp.sum(jnp.where(cell_y == lane_y, by_x, 0.0), axis=1, keepdims=True)
        picked[inputs] = jnp.broadcast_to(slant, (slots, levels))
        for k in range(half):
            block = picked[:, k * share:(k + 1) * share, :]
            send_ref[parity, k] = block.reshape(fields * share, levels).astype(BF16)

    def cells_of(first, count):
        block = air_ref[:, pl.ds(first, count), :]
        return pltpu.einshape("fcl->cfl", block).reshape(count * fields, levels).astype(BF16)

    for x in range(halo):
        xlow_ref[x] = cells_of(x * width_y, width_y)
        xhigh_ref[x] = cells_of((width_x - halo + x) * width_y, width_y)
    for x in range(width_x):
        low = cells_of(x * width_y, 8)
        high = cells_of((x + 1) * width_y - 8, 8)
        ylow_ref[x] = low[:halo * fields]
        yhigh_ref[x] = high[(8 - halo) * fields:]


def exchange_kernel(cols, specs, halo, send_ref, xlow_ref, xhigh_ref, ylow_ref, yhigh_ref,
                    feat_ref, xl_ref, xh_ref, yl_ref, yh_ref,
                    pair_in, merged, group_in, send_sem, recv_sem, group_send, group_recv,
                    spec_send, spec_recv):
    col, spec = lax.axis_index("cols"), lax.axis_index("spec")
    half = cols // 2
    parity, k = lax.rem(col, 2), lax.div(col, 2)
    partner = col + 1 - 2 * parity
    east, west = lax.rem(col + 1, cols), lax.rem(col + cols - 1, cols)
    north, south = lax.rem(spec + 1, specs), lax.rem(spec + specs - 1, specs)
    barrier = pltpu.get_barrier_semaphore()
    peers = [(partner, spec), (east, spec), (west, spec)]
    peers += [(2 * lax.rem(k + d, half) + parity, spec) for d in range(1, half)]
    peers += [(col, lax.rem(spec + d, specs)) for d in range(1, specs)]
    for peer in peers:
        pl.semaphore_signal(barrier, inc=1, device_id=peer, device_id_type=MESH)
    pl.semaphore_wait(barrier, len(peers))

    def copy(src, dst, number, peer):
        return pltpu.make_async_remote_copy(
            src_ref=src, dst_ref=dst, send_sem=send_sem.at[number],
            recv_sem=recv_sem.at[number], device_id=peer, device_id_type=MESH,
        )

    width_x = ylow_ref.shape[0]
    rows = ylow_ref.shape[1]
    row_end = xlow_ref.shape[1]
    pair = copy(send_ref.at[1 - parity], pair_in, 0, (partner, spec))
    pair.start()
    sides = [
        copy(xlow_ref, xh_ref, 1, (west, spec)),
        copy(xhigh_ref, xl_ref, 2, (east, spec)),
        copy(ylow_ref, yh_ref.at[pl.ds(halo, width_x)], 3, (col, south)),
        copy(yhigh_ref, yl_ref.at[pl.ds(halo, width_x)], 4, (col, north)),
    ]
    pair.wait()
    merged[...] = send_ref[parity] + pair_in[...]
    groups = []
    for d in range(1, half):
        other = lax.rem(k + d, half)
        groups.append(pltpu.make_async_remote_copy(
            src_ref=merged.at[other], dst_ref=group_in.at[d - 1],
            send_sem=group_send.at[d - 1], recv_sem=group_recv.at[d - 1],
            device_id=(2 * other + parity, spec), device_id_type=MESH,
        ))
    for one in groups:
        one.start()
    for one in sides:
        one.start()
    for one in groups:
        one.wait()
    total = merged[k]
    for d in range(1, half):
        total = total + group_in[d - 1]
    feat_ref[spec] = total
    spreads = []
    for d in range(1, specs):
        spreads.append(pltpu.make_async_remote_copy(
            src_ref=feat_ref.at[spec], dst_ref=feat_ref.at[spec],
            send_sem=spec_send.at[d - 1], recv_sem=spec_recv.at[d - 1],
            device_id=(col, lax.rem(spec + d, specs)), device_id_type=MESH,
        ))
    for one in spreads:
        one.start()
    for one in sides:
        one.wait()
    corners = [
        copy(xl_ref.at[:, pl.ds(0, rows)], yh_ref.at[pl.ds(0, halo)], 5, (col, south)),
        copy(xh_ref.at[:, pl.ds(0, rows)], yh_ref.at[pl.ds(halo + width_x, halo)], 6, (col, south)),
        copy(xl_ref.at[:, pl.ds(row_end - rows, rows)], yl_ref.at[pl.ds(0, halo)], 7, (col, north)),
        copy(xh_ref.at[:, pl.ds(row_end - rows, rows)], yl_ref.at[pl.ds(halo + width_x, halo)], 8,
             (col, north)),
    ]
    for one in corners:
        one.start()
    for d in range(1, specs):
        spreads[d - 1].wait_send()
        source = lax.rem(spec + specs - d, specs)
        pltpu.make_async_remote_copy(
            src_ref=feat_ref.at[source], dst_ref=feat_ref.at[source],
            send_sem=spec_send.at[d - 1], recv_sem=spec_recv.at[d - 1],
            device_id=(col, lax.rem(spec + d, specs)), device_id_type=MESH,
        ).wait_recv()
    for one in corners:
        one.wait()


def silu(value):
    half = 0.5 * value
    return half + half * jnp.tanh(half)


def radiate_kernel(share, feat_ref, in_weight_ref, in_bias_ref, mid_weight_ref, mid_bias_ref,
                   out_weight_ref, out_bias_ref, absorption_ref, flux_ref, heat_ref,
                   feats, hidden, upward, down, heat):
    specs, rows, levels = feat_ref.shape
    fields = rows // share
    columns = specs * share
    block_levels = out_weight_ref.shape[0]
    step = pl.program_id(0)
    slant = jnp.concatenate(
        [feat_ref[s].astype(F32)[(fields - 1) * share:] for s in range(specs)], axis=0
    )[:, :1]

    @pl.when(step == 0)
    def _():
        for s in range(specs):
            feats[s * rows:(s + 1) * rows, :] = feat_ref[s].astype(F32)
        weight = jnp.concatenate(
            [in_weight_ref[...].astype(F32), jnp.zeros((1, in_weight_ref.shape[1]), F32)], axis=0
        ).astype(BF16)
        mid_weight = mid_weight_ref[...]
        in_bias, mid_bias = in_bias_ref[...], mid_bias_ref[...]

        @pl.loop(0, columns // 8)
        def _(group):
            s = group // (share // 8)
            first = s * rows + (group - s * (share // 8)) * 8
            ones = []
            for j in range(8):
                column = feats[pl.ds(first + j, fields, stride=share), :].astype(BF16)
                summed = lax.dot_general(
                    column, weight, (((0,), (0,)), ((), ())), preferred_element_type=F32
                )
                ones.append(silu(summed + in_bias).astype(BF16))
            second = jnp.dot(
                jnp.concatenate(ones, axis=0), mid_weight, preferred_element_type=F32
            )
            second = silu(second + mid_bias)
            for j in range(8):
                hidden[pl.ds(group * 8 + j, levels, stride=columns), :] = (
                    second[j * levels:(j + 1) * levels]
                )

        down[...] = flux_ref[...] * slant
        heat[...] = jnp.zeros_like(heat)

    absorption = absorption_ref[...]
    down_rate = -(absorption / slant)
    up_rate = -DIFFUSIVITY * absorption
    out_bias = out_bias_ref[...]
    lane = lax.broadcasted_iota(jnp.int32, (columns, levels), 1)

    @pl.loop(0, block_levels // 8)
    def _(part):
        now = down[...]
        total = heat[...]
        for j in range(8):
            local = part * 8 + j
            level = step * block_levels + local
            start = pl.multiple_of(level * columns, 8)
            two = hidden[pl.ds(start, columns), :].astype(BF16)
            logits = lax.dot_general(
                two, out_weight_ref[local], (((1,), (1,)), ((), ())), preferred_element_type=F32
            ) + out_bias
            small = jnp.exp(-jnp.abs(logits))
            soft = jnp.maximum(logits, 0.0) + jnp.where(
                small < 1e-3, small - 0.5 * small * small, jnp.log(1.0 + small)
            )
            below = now * jnp.exp(down_rate * soft)
            upward[level] = jnp.exp(up_rate * soft)
            gone = jnp.sum(now - below, axis=1, keepdims=True)
            total = jnp.where(lane == level, gone, total)
            now = below
        down[...] = now
        heat[...] = total

    @pl.when(step == pl.num_programs(0) - 1)
    def _():
        down[...] = ALBEDO * down[...]

        @pl.loop(0, levels // 8)
        def _(part):
            now = down[...]
            total = heat[...]
            for j in range(8):
                level = levels - 1 - (part * 8 + j)
                above = now * upward[level]
                gone = jnp.sum(now - above, axis=1, keepdims=True)
                total = jnp.where(lane == level, total + gone, total)
                now = above
            down[...] = now
            heat[...] = total

        heat_ref[...] = heat[...]


def gather_kernel(cols, specs, share, part_ref, heat_ref, spec_in, spec_send, spec_recv,
                  group_send, group_recv, pair_send, pair_recv):
    col, spec = lax.axis_index("cols"), lax.axis_index("spec")
    half = cols // 2
    parity, k = lax.rem(col, 2), lax.div(col, 2)
    partner = col + 1 - 2 * parity
    barrier = pltpu.get_barrier_semaphore()
    peers = [(partner, spec)]
    peers += [(2 * lax.rem(k + d, half) + parity, spec) for d in range(1, half)]
    peers += [(col, lax.rem(spec + d, specs)) for d in range(1, specs)]
    for peer in peers:
        pl.semaphore_signal(barrier, inc=1, device_id=peer, device_id_type=MESH)
    pl.semaphore_wait(barrier, len(peers))
    copies = []
    for d in range(1, specs):
        other = lax.rem(spec + d, specs)
        copies.append(pltpu.make_async_remote_copy(
            src_ref=part_ref.at[other], dst_ref=spec_in.at[d - 1],
            send_sem=spec_send.at[d - 1], recv_sem=spec_recv.at[d - 1],
            device_id=(col, other), device_id_type=MESH,
        ))
    for one in copies:
        one.start()
    for one in copies:
        one.wait()
    total = part_ref[spec]
    for d in range(1, specs):
        total = total + spec_in[d - 1]
    heat_ref[parity, k] = total
    groups = []
    for d in range(1, half):
        groups.append(pltpu.make_async_remote_copy(
            src_ref=heat_ref.at[parity, k], dst_ref=heat_ref.at[parity, k],
            send_sem=group_send.at[d - 1], recv_sem=group_recv.at[d - 1],
            device_id=(2 * lax.rem(k + d, half) + parity, spec), device_id_type=MESH,
        ))
    for one in groups:
        one.start()
    for d in range(1, half):
        groups[d - 1].wait_send()
        source = lax.rem(k + half - d, half)
        pltpu.make_async_remote_copy(
            src_ref=heat_ref.at[parity, source], dst_ref=heat_ref.at[parity, source],
            send_sem=group_send.at[d - 1], recv_sem=group_recv.at[d - 1],
            device_id=(2 * lax.rem(k + d, half) + parity, spec), device_id_type=MESH,
        ).wait_recv()
    pair = pltpu.make_async_remote_copy(
        src_ref=heat_ref.at[parity], dst_ref=heat_ref.at[parity],
        send_sem=pair_send, recv_sem=pair_recv,
        device_id=(partner, spec), device_id_type=MESH,
    )
    pair.start()
    pair.wait_send()
    pltpu.make_async_remote_copy(
        src_ref=heat_ref.at[1 - parity], dst_ref=heat_ref.at[1 - parity],
        send_sem=pair_send, recv_sem=pair_recv,
        device_id=(partner, spec), device_id_type=MESH,
    ).wait_recv()


def finish_kernel(share, halo, width_y, place_ref, air_ref, xl_ref, xh_ref, yl_ref, yh_ref,
                  courant_x_ref, courant_y_ref, index_ref, count_ref, heat_ref,
                  state_ref, grid_ref, first, second):
    fields, cells, levels = air_ref.shape
    width_x = cells // width_y
    col, spec = place_ref[0], place_ref[1]
    half = heat_ref.shape[1]
    wide_x, wide_y = width_x + 2 * halo, width_y + 2 * halo

    @pl.loop(0, width_x)
    def _(x):
        block = air_ref[:, pl.ds(pl.multiple_of(x * width_y, 8), width_y), :]
        first[x + halo, halo:halo + width_y] = pltpu.einshape("fcl->cfl", block)

    def unpacked(value, count):
        return value.astype(F32).reshape(count, fields, levels)

    for x in range(halo):
        first[x, halo:halo + width_y] = unpacked(xl_ref[x], width_y)
        first[halo + width_x + x, halo:halo + width_y] = unpacked(xh_ref[x], width_y)

    @pl.loop(0, wide_x)
    def _(x):
        first[x, 0:halo] = unpacked(yl_ref[x], halo)
        first[x, halo + width_y:wide_y] = unpacked(yh_ref[x], halo)

    rate_x, rate_y = courant_x_ref[...], courant_y_ref[...]
    spread_x = 0.5 * rate_x * rate_x + DIFFUSION
    spread_y = 0.5 * rate_y * rate_y + DIFFUSION

    def wide(row):
        return jnp.broadcast_to(row, (fields, levels))[None]

    keep = wide(1.0 - 2.0 * spread_x - 2.0 * spread_y)
    from_east, from_west = wide(spread_x - 0.5 * rate_x), wide(spread_x + 0.5 * rate_x)
    from_north, from_south = wide(spread_y - 0.5 * rate_y), wide(spread_y + 0.5 * rate_y)
    buffers = (first, second)
    for section in range(SECTIONS):
        source, target = buffers[section % 2], buffers[(section + 1) % 2]
        low, high = section + 1, wide_y - section - 1

        @pl.loop(section + 1, wide_x - section - 1)
        def _(x):
            target[x, low:high] = (
                keep * source[x, low:high]
                + from_east * source[x + 1, low:high]
                + from_west * source[x - 1, low:high]
                + from_north * source[x, low + 1:high + 1]
                + from_south * source[x, low - 1:high - 1]
            )

    done = buffers[SECTIONS % 2]
    grid = jnp.zeros((cells, levels), F32)
    for parity in range(2):
        cell = cell_column(
            rank_column(parity, half, share), count_ref[...], index_ref[0], spec, col
        )
        slots = cell.shape[0]
        lane = lax.broadcasted_iota(jnp.int32, (slots, cells), 1).astype(F32)
        choose = jnp.where(cell == lane, 1.0, 0.0).astype(BF16)
        rows = heat_ref[parity].reshape(slots, levels)
        upper = rows.astype(BF16)
        lower = (rows - upper.astype(F32)).astype(BF16)
        for piece in (upper, lower):
            grid = grid + lax.dot_general(
                choose, piece, (((0,), (0,)), ((), ())), preferred_element_type=F32
            )
    grid_ref[...] = grid

    @pl.loop(0, width_x)
    def _(x):
        block = done[x + halo, halo:halo + width_y]
        start = pl.multiple_of(x * width_y, 8)
        state_ref[:, pl.ds(start, width_y), :] = pltpu.einshape("cfl->fcl", block)
        state_ref[0, pl.ds(start, width_y), :] += grid_ref[pl.ds(start, width_y), :]


def on_device(
    air_state,
    courant_x,
    courant_y,
    cos_zenith,
    sun_index,
    sun_count,
    in_weight,
    in_bias,
    mid_weight,
    mid_bias,
    out_weight,
    out_bias,
    absorption,
    solar_flux,
):
    fields, width_x, width_y, levels = air_state.shape
    cells = width_x * width_y
    cols, specs = lax.axis_size("cols"), lax.axis_size("spec")
    half = cols // 2
    share = sun_index.shape[2] // 4
    halo = SECTIONS
    block_rows = fields * share
    air = air_state.reshape(fields, cells, levels)
    place = jnp.stack([lax.axis_index("cols"), lax.axis_index("spec")]).astype(jnp.int32)
    smem = pl.BlockSpec(memory_space=pltpu.SMEM)
    vmem = pl.BlockSpec(memory_space=pltpu.VMEM)
    dma = pltpu.SemaphoreType.DMA
    x_halo = jax.ShapeDtypeStruct((halo, width_y * fields, levels), BF16)
    params = pltpu.CompilerParams(vmem_limit_bytes=VMEM_LIMIT)

    packed = pl.pallas_call(
        functools.partial(pack_kernel, share, half, width_y, halo),
        out_shape=(
            jax.ShapeDtypeStruct((2, half, block_rows, levels), BF16),
            x_halo,
            x_halo,
            jax.ShapeDtypeStruct((width_x, halo * fields, levels), BF16),
            jax.ShapeDtypeStruct((width_x, halo * fields, levels), BF16),
        ),
        in_specs=[smem, vmem, vmem, vmem, vmem],
        out_specs=(vmem,) * 5,
        scratch_shapes=[pltpu.VMEM((fields, half * share, levels), F32)],
        compiler_params=params,
        name="pack",
    )(place, air, cos_zenith, sun_index, sun_count)

    y_halo = jax.ShapeDtypeStruct((width_x + 2 * halo, halo * fields, levels), BF16)
    features, x_low, x_high, y_low, y_high = pl.pallas_call(
        functools.partial(exchange_kernel, cols, specs, halo),
        out_shape=(
            jax.ShapeDtypeStruct((specs, block_rows, levels), BF16),
            x_halo,
            x_halo,
            y_halo,
            y_halo,
        ),
        in_specs=[vmem] * 5,
        out_specs=(vmem,) * 5,
        scratch_shapes=[
            pltpu.VMEM((half, block_rows, levels), BF16),
            pltpu.VMEM((half, block_rows, levels), BF16),
            pltpu.VMEM((half - 1, block_rows, levels), BF16),
            dma((9,)),
            dma((9,)),
            dma((half - 1,)),
            dma((half - 1,)),
            dma((specs - 1,)),
            dma((specs - 1,)),
        ],
        compiler_params=pltpu.CompilerParams(
            vmem_limit_bytes=VMEM_LIMIT, collective_id=0, has_side_effects=True
        ),
        name="exchange",
    )(*packed)

    columns = specs * share
    points = out_weight.shape[1]
    block_levels = 16

    def whole(shape):
        return pl.BlockSpec(shape, lambda i: (0,) * len(shape))

    operands = (
        features,
        in_weight,
        in_bias.reshape(1, -1),
        mid_weight,
        mid_bias.reshape(1, -1),
        out_weight,
        out_bias.reshape(1, -1),
        absorption.reshape(1, -1),
        solar_flux.reshape(1, -1),
    )
    specs_in = [whole(a.shape) for a in operands]
    specs_in[5] = pl.BlockSpec((block_levels,) + out_weight.shape[1:], lambda i: (i, 0, 0))
    partial_heat = pl.pallas_call(
        functools.partial(radiate_kernel, share),
        out_shape=jax.ShapeDtypeStruct((columns, levels), F32),
        grid=(levels // block_levels,),
        in_specs=specs_in,
        out_specs=whole((columns, levels)),
        scratch_shapes=[
            pltpu.VMEM((specs * block_rows, levels), F32),
            pltpu.VMEM((levels * columns, mid_weight.shape[1]), F32),
            pltpu.VMEM((levels, columns, points), F32),
            pltpu.VMEM((columns, points), F32),
            pltpu.VMEM((columns, levels), F32),
        ],
        compiler_params=params,
        name="radiate",
    )(*operands)

    heats = pl.pallas_call(
        functools.partial(gather_kernel, cols, specs, share),
        out_shape=jax.ShapeDtypeStruct((2, half, share, levels), F32),
        in_specs=[vmem],
        out_specs=vmem,
        scratch_shapes=[
            pltpu.VMEM((specs - 1, share, levels), F32),
            dma((specs - 1,)),
            dma((specs - 1,)),
            dma((half - 1,)),
            dma((half - 1,)),
            dma,
            dma,
        ],
        compiler_params=pltpu.CompilerParams(
            vmem_limit_bytes=VMEM_LIMIT, collective_id=1, has_side_effects=True
        ),
        name="gather",
    )(partial_heat.reshape(specs, share, levels))

    wide = (width_x + 2 * halo, width_y + 2 * halo, fields, levels)
    state, grid = pl.pallas_call(
        functools.partial(finish_kernel, share, halo, width_y),
        out_shape=(
            jax.ShapeDtypeStruct((fields, cells, levels), F32),
            jax.ShapeDtypeStruct((cells, levels), F32),
        ),
        in_specs=[smem] + [vmem] * 10,
        out_specs=(vmem, vmem),
        scratch_shapes=[pltpu.VMEM(wide, F32), pltpu.VMEM(wide, F32)],
        compiler_params=params,
        name="finish",
    )(place, air, x_low, x_high, y_low, y_high, courant_x.reshape(1, -1),
      courant_y.reshape(1, -1), sun_index, sun_count, heats)
    return (
        state.reshape(air_state.shape),
        grid.reshape(width_x, width_y, levels),
    )


def solution(mesh):
    placed = (
        P(None, "cols", "spec", None),
        P(),
        P(),
        P("cols", "spec"),
        P("cols", "spec", None),
        P(),
        P(),
        P(),
        P(),
        P(),
        P(None, "spec", None),
        P("spec"),
        P("spec"),
        P("spec"),
    )
    return jax.shard_map(
        on_device,
        mesh=mesh,
        in_specs=placed,
        out_specs=(P(None, "cols", "spec", None), P("cols", "spec", None)),
        check_vma=False,
    )
```

time: 183 us -> 70.3 us (0.38)
  Pallas kernels: 0 us -> 68.6 us
  local copies, waits for them, and re-layouts: 46.2 us -> 0 us
  starting transfers between devices: 35.5 us -> 0 us
  other arithmetic: 27.9 us -> 0.65 us
  waiting for transfers between devices: 24.5 us -> 0 us
  matrix products: 21.2 us -> 0 us
  between operations: 16.6 us -> 0.65 us
  blocking collectives: 9.62 us -> 0 us
    pallas_call x0 -> x5, Pallas kernels: none -> 68.6 us  [the longest x1 26.6 us: on_device(): pl.pallas_call(functools.partial(exchange_kernel, cols, specs, halo), out...]
    dot_general x9 -> x0, matrix products: 21.2 us -> none  [the longest x3 13.5 us: radiate_block(): jnp.einsum('lgh,lnh->lgn', out_weight, hidden_two, preferred_element_type...]
    ppermute x16 -> x0, starting transfers between devices: 20.5 us -> none  [the longest x8 16.9 us: padded_2(): lax.ppermute(head, axis, [((i + 1) % count, i) for i in range(count)])]
    all_to_all x3 -> x0, starting transfers between devices: 15 us -> none  [the longest x1 5.59 us: on_device(): lax.all_to_all(send_back, 'cols', split_axis=0, concat_axis=0, tiled=True)]
    unnamed x68 -> x0, local copies, waits for them, and re-layouts: 13 us -> none
    gather x13 -> x0, local copies, waits for them, and re-layouts: 12.8 us -> none  [the longest x5 3.49 us: on_device(): anchor = jnp.searchsorted(row_ends, slot_rank, side='right')]
    ppermute x16 -> x0, waiting for transfers between devices: 11.7 us -> none  [the longest x8 8.17 us: padded_2(): lax.ppermute(tail, axis, [(i, (i + 1) % count) for i in range(count)])]
    add x10 -> x0, other arithmetic: 10.7 us -> none  [the longest x4 8.75 us: section_update(): centre - 0.5 * courant_x * (eastern - western)]
  transfers between devices with their start and end apart: 20 -> 0, of which waited for: 8 -> 0; matrix products, arithmetic and copies ran while one was open for 40% -> 0% of each run, Pallas kernels for 0% -> 0%
where the time goes in v1:
time: 70.3 us; the launch traced here: 69.9 us
  Pallas kernels  68.6 us (98%)
    pallas_call x1, Pallas kernels, on_device(): pl.pallas_call(functools.partial(exchange_kernel, cols, specs, halo), out...  26.6 us
    pallas_call x1, Pallas kernels, on_device(): pl.pallas_call(functools.partial(radiate_kernel, share), out_shape=jax.Sh...  15.4 us
    pallas_call x1, Pallas kernels, on_device(): pl.pallas_call(functools.partial(gather_kernel, cols, specs, share), out_...  13.7 us
    pallas_call x1, Pallas kernels, on_device(): pl.pallas_call(functools.partial(finish_kernel, share, halo, width_y), ou...  8.87 us
    pallas_call x1, Pallas kernels, on_device(): pl.pallas_call(functools.partial(pack_kernel, share, half, width_y, halo)...  4.04 us

profile of v1, /device:TPU:0, one launch (start us, length us, event | category | flops | bytes accessed | tf_op | source)
XLA Modules:
  0.0 69.9 jit_solution(12851610992017868285)
XLA Ops:
  0.6 0.7 pad_add_fusion.place_ref
  1.3 4.0 %pack.1 = (bf16[2,8,192,128]{3,2,1,0:T(8,128)(2,1)}, bf16[4,256,128]{2,1,0:T(8,128)(2,1)}, bf16[4,256,128]{2,1,0:T(8,128)(2,1)}, bf16[16,32,128]{2,1,0:T(8,128)(2,1)}, bf16[16,32,128]{2,1,0:T(8,128)(2,1)}) custom-call(s32[2]{0:T(128)} %pad_add_fusion.place_ref, f32[8,512,128]{2,1,0:T(8,128)} %bitcast.13, f32[16,32]{1,0:T(8,128)} %cos_ref.1, ...), custom_call_target="tpu_custom_call" | custom-call | tf_op jit(solution)/shard_map/pack/pallas_call | solution.py:440
  5.3 26.6 %exchange.1 = (bf16[2,192,128]{2,1,0:T(8,128)(2,1)}, bf16[4,256,128]{2,1,0:T(8,128)(2,1)}, bf16[4,256,128]{2,1,0:T(8,128)(2,1)}, bf16[24,32,128]{2,1,0:T(8,128)(2,1)}, bf16[24,32,128]{2,1,0:T(8,128)(2,1)}) custom-call(bf16[2,8,192,128]{3,2,1,0:T(8,128)(2,1)} %get-tuple-element.14.send_ref, bf16[4,256,128]{2,1,0:T(8,128)(2,1)} %get-tuple-element.15.xlow_ref, ...), custom_call_target="tpu_custom_call" | custom-call | tf_op jit(solution)/shard_map/exchange/pallas_call | solution.py:457
  31.9 15.4 %radiate.1 = f32[48,128]{1,0:T(8,128)} custom-call(bf16[2,192,128]{2,1,0:T(8,128)(2,1)} %get-tuple-element.23.feat_ref, bf16[7,128]{1,0:T(8,128)(2,1)} %in_weight_ref.1, f32[1,128]{1,0:T(1,128)} %bitcast.18, bf16[128,128]{1,0:T(8,128)(2,1)} %mid_weight_ref.1, f32[1,128]{1,0:T(1,128)} %bitcast.19, bf16[128,128,128]{2,1,0:T(8,128)(2,1)} %out_weight_ref.1, ...), custom_call_target="tpu_custom_call" | custom-call | tf_op jit(solution)/shard_map/radiate/pallas_call | solution.py:505
  47.3 13.7 %gather.1.heat_ref = f32[2,8,24,128]{3,2,1,0:T(8,128)} custom-call(f32[2,24,128]{2,1,0:T(8,128)} %bitcast.15), custom_call_target="tpu_custom_call" | custom-call | tf_op jit(solution)/shard_map/gather/pallas_call | solution.py:522
  61.0 8.9 %finish.1 = (f32[8,512,128]{2,1,0:T(8,128)}, f32[512,128]{1,0:T(8,128)}) custom-call(s32[2]{0:T(128)} %pad_add_fusion.place_ref, f32[8,512,128]{2,1,0:T(8,128)} %bitcast.14, bf16[4,256,128]{2,1,0:T(8,128)(2,1)} %get-tuple-element.19.xl_ref, bf16[4,256,128]{2,1,0:T(8,128)(2,1)} %get-tuple-element.20.xh_ref, bf16[24,32,128]{2,1,0:T(8,128)(2,1)} %get-tuple-element.21.yl_ref, ...), custom_call_target="tpu_custom_call" | custom-call | tf_op jit(solution)/shard_map/finish/pallas_call | solution.py:543

commit v2 on v0

v2 whole, which is shorter than its diff:
```python
import functools

import jax
import jax.numpy as jnp
from jax import lax
from jax.experimental import pallas as pl
from jax.experimental.pallas import tpu as pltpu
from jax.sharding import PartitionSpec as P

SECTIONS = 4
DIFFUSION = 0.05
ALBEDO = 0.3
DIFFUSIVITY = 1.66
MESH = pl.DeviceIdType.MESH
F32 = jnp.float32
BF16 = jnp.bfloat16
VMEM_LIMIT = 56 * 1024 * 1024


def cell_column(ranks, counts, index_row, spec, col):
    row = lax.broadcasted_iota(jnp.int32, counts.shape, 0)
    column = lax.broadcasted_iota(jnp.int32, counts.shape, 1)
    values = jnp.where(row == spec, counts, 0).astype(F32)
    offset = jnp.sum(jnp.where(column < col, values, 0.0), axis=(0, 1), keepdims=True)
    own = jnp.sum(jnp.where(column == col, values, 0.0), axis=(0, 1), keepdims=True)
    place = lax.broadcasted_iota(jnp.int32, (1, index_row.shape[1]), 1).astype(F32)
    table = jnp.where(place < own, index_row.astype(F32) + 1.0, 0.0)
    found = jnp.where(ranks - offset == place, table, 0.0)
    return jnp.sum(found, axis=1, keepdims=True) - 1.0


def rank_column(firsts, share):
    within = lax.broadcasted_iota(jnp.int32, (share, 1), 0)
    return jnp.concatenate([(first * share + within).astype(F32) for first in firsts], axis=0)


def silu(value):
    half = 0.5 * value
    return half + half * jnp.tanh(half)


def remote(src, dst, send, recv, peer):
    return pltpu.make_async_remote_copy(
        src_ref=src, dst_ref=dst, send_sem=send, recv_sem=recv, device_id=peer, device_id_type=MESH
    )


def main_kernel(cols, specs, share, halo, width_y,
                air_ref, cos_ref, index_ref, count_ref, courant_x_ref, courant_y_ref,
                in_weight_ref, in_bias_ref, mid_weight_ref, mid_bias_ref, out_weight_ref,
                out_bias_ref, absorption_ref, flux_ref,
                state_ref, heat_ref,
                send_ref, xlow_ref, xhigh_ref, ylow_ref, yhigh_ref, picked,
                feat_ref, xl_ref, xh_ref, yl_ref, yh_ref,
                pair_in, merged, next_in, narrowed, group_in,
                out_weight, feats, hidden, upward, part_ref, spec_in, first, second,
                weight_sem, send_sem, recv_sem, group_send, group_recv, spec_send, spec_recv,
                back_send, back_recv, heat_send, heat_recv):
    fields, cells, levels = air_ref.shape
    width_x = cells // width_y
    inputs = fields - 1
    wide_x, wide_y = width_x + 2 * halo, width_y + 2 * halo
    columns = specs * share
    block = fields * share
    col, spec = lax.axis_index("cols"), lax.axis_index("spec")
    half, quarter = cols // 2, cols // 4
    parity, k = lax.rem(col, 2), lax.div(col, 2)
    bit, kk = lax.rem(k, 2), lax.div(k, 2)
    partner = col + 1 - 2 * parity
    across = col + 2 - 4 * bit
    east, west = lax.rem(col + 1, cols), lax.rem(col + cols - 1, cols)
    north, south = lax.rem(spec + 1, specs), lax.rem(spec + specs - 1, specs)
    barrier = pltpu.get_barrier_semaphore()
    peers = [(partner, spec), (east, spec), (west, spec)]
    peers += [(2 * lax.rem(k + d, half) + parity, spec) for d in range(1, half)]
    peers += [(col, lax.rem(spec + d, specs)) for d in range(1, specs)]
    for peer in peers:
        pl.semaphore_signal(barrier, inc=1, device_id=peer, device_id_type=MESH)
    fetch = pltpu.make_async_copy(out_weight_ref, out_weight, weight_sem)
    fetch.start()

    def copy(src, dst, number, peer):
        return remote(src, dst, send_sem.at[number], recv_sem.at[number], peer)

    counts, index_row = count_ref[...], index_ref[0]

    def pack(which):
        ranks = rank_column(
            [4 * c + 2 * b + which for b in range(2) for c in range(quarter)], share
        )
        cell = cell_column(ranks, counts, index_row, spec, col)
        slots = cell.shape[0]
        lane = lax.broadcasted_iota(jnp.int32, (slots, cells), 1).astype(F32)
        choose = jnp.where(cell == lane, 1.0, 0.0).astype(BF16)
        for i in range(inputs):
            picked[i] = jnp.dot(choose, air_ref[i].astype(BF16), preferred_element_type=F32)
        cell_x = jnp.floor((cell + 0.5) * (1.0 / width_y))
        cell_y = cell - cell_x * width_y
        lane_x = lax.broadcasted_iota(jnp.int32, (slots, width_x), 1).astype(F32)
        lane_y = lax.broadcasted_iota(jnp.int32, (slots, width_y), 1).astype(F32)
        by_x = jnp.dot(
            jnp.where(cell_x == lane_x, 1.0, 0.0).astype(BF16),
            cos_ref[...].astype(BF16),
            preferred_element_type=F32,
        )
        slant = jnp.sum(jnp.where(cell_y == lane_y, by_x, 0.0), axis=1, keepdims=True)
        picked[inputs] = jnp.broadcast_to(slant, (slots, levels))
        blocks = []
        for at in range(half):
            piece = picked[:, at * share:(at + 1) * share, :]
            blocks.append(piece.reshape(block, levels).astype(BF16)[None])
        return jnp.concatenate(blocks, axis=0).reshape(2, quarter, block, levels)

    send_ref[...] = pack(1 - parity)
    pl.semaphore_wait(barrier, len(peers))
    pair = copy(send_ref, pair_in, 0, (partner, spec))
    pair.start()
    merged[...] = pack(parity)
    pair.wait()
    merged[...] = merged[...] + pair_in[...]
    over = copy(merged.at[1 - bit], next_in, 9, (across, spec))
    over.start()

    def cells_of(start, count):
        piece = air_ref[:, pl.ds(start, count), :]
        return pltpu.einshape("fcl->cfl", piece).reshape(count * fields, levels).astype(BF16)

    for x in range(halo):
        xlow_ref[x] = cells_of(x * width_y, width_y)
        xhigh_ref[x] = cells_of((width_x - halo + x) * width_y, width_y)
    over.wait()
    narrowed[...] = merged[bit] + next_in[...]
    groups = []
    for d in range(1, quarter):
        other = lax.rem(kk + d, quarter)
        groups.append(remote(
            narrowed.at[other], group_in.at[d - 1], group_send.at[d - 1], group_recv.at[d - 1],
            (4 * other + 2 * bit + parity, spec),
        ))
    for one in groups:
        one.start()

    @pl.loop(0, width_x)
    def _(x):
        low = cells_of(pl.multiple_of(x * width_y, 8), 8)
        high = cells_of(pl.multiple_of(x * width_y + width_y - 8, 8), 8)
        ylow_ref[x] = low[:halo * fields]
        yhigh_ref[x] = high[(8 - halo) * fields:]

    for one in groups:
        one.wait()
    total = narrowed[kk]
    for d in range(1, quarter):
        total = total + group_in[d - 1]
    feat_ref[spec] = total
    spreads = []
    for d in range(1, specs):
        spreads.append(remote(
            feat_ref.at[spec], feat_ref.at[spec], spec_send.at[d - 1], spec_recv.at[d - 1],
            (col, lax.rem(spec + d, specs)),
        ))
    for one in spreads:
        one.start()
    rows = ylow_ref.shape[1]
    row_end = xlow_ref.shape[1]
    sides = [
        copy(xlow_ref, xh_ref, 1, (west, spec)),
        copy(xhigh_ref, xl_ref, 2, (east, spec)),
        copy(ylow_ref, yh_ref.at[pl.ds(halo, width_x)], 3, (col, south)),
        copy(yhigh_ref, yl_ref.at[pl.ds(halo, width_x)], 4, (col, north)),
    ]
    for one in sides:
        one.start()

    @pl.loop(0, width_x)
    def _(x):
        piece = air_ref[:, pl.ds(pl.multiple_of(x * width_y, 8), width_y), :]
        first[x + halo, halo:halo + width_y] = pltpu.einshape("fcl->cfl", piece)

    for d in range(1, specs):
        spreads[d - 1].wait_send()
        source = lax.rem(spec + specs - d, specs)
        remote(
            feat_ref.at[source], feat_ref.at[source], spec_send.at[d - 1], spec_recv.at[d - 1],
            (col, lax.rem(spec + d, specs)),
        ).wait_recv()

    for s in range(specs):
        feats[s * block:(s + 1) * block, :] = feat_ref[s].astype(F32)
    slant = jnp.concatenate(
        [feats[s * block + inputs * share:(s + 1) * block, :] for s in range(specs)], axis=0
    )[:, :1]
    weight = jnp.concatenate(
        [in_weight_ref[...].astype(F32), jnp.zeros((1, in_weight_ref.shape[1]), F32)], axis=0
    ).astype(BF16)
    mid_weight = mid_weight_ref[...]
    in_bias, mid_bias = in_bias_ref[...], mid_bias_ref[...]

    for s in range(specs):
        @pl.loop(0, share // 8)
        def _(group):
            ones = []
            for j in range(8):
                column = feats[pl.ds(s * block + group * 8 + j, fields, stride=share), :]
                summed = lax.dot_general(
                    column.astype(BF16), weight, (((0,), (0,)), ((), ())),
                    preferred_element_type=F32,
                )
                ones.append(silu(summed + in_bias).astype(BF16))
            middle = jnp.dot(
                jnp.concatenate(ones, axis=0), mid_weight, preferred_element_type=F32
            )
            middle = silu(middle + mid_bias)
            for j in range(8):
                start = s * share + group * 8 + j
                hidden[pl.ds(start, levels, stride=columns), :] = (
                    middle[j * levels:(j + 1) * levels]
                )

    for one in sides:
        one.wait()
    corners = [
        copy(xl_ref.at[:, pl.ds(0, rows)], yh_ref.at[pl.ds(0, halo)], 5, (col, south)),
        copy(xh_ref.at[:, pl.ds(0, rows)], yh_ref.at[pl.ds(halo + width_x, halo)], 6, (col, south)),
        copy(xl_ref.at[:, pl.ds(row_end - rows, rows)], yl_ref.at[pl.ds(0, halo)], 7, (col, north)),
        copy(xh_ref.at[:, pl.ds(row_end - rows, rows)], yl_ref.at[pl.ds(halo + width_x, halo)], 8,
             (col, north)),
    ]
    for one in corners:
        one.start()
    fetch.wait()

    absorption = absorption_ref[...]
    down_rate = -(absorption / slant)
    up_rate = -DIFFUSIVITY * absorption
    out_bias = out_bias_ref[...]
    lane = lax.broadcasted_iota(jnp.int32, (columns, levels), 1)
    unroll = 16

    def downward(part, carry):
        now, kept = carry
        for j in range(unroll):
            level = part * unroll + j
            start = pl.multiple_of(level * columns, 8)
            two = hidden[pl.ds(start, columns), :].astype(BF16)
            logits = lax.dot_general(
                two, out_weight[level], (((1,), (1,)), ((), ())), preferred_element_type=F32
            ) + out_bias
            small = jnp.exp(-jnp.abs(logits))
            soft = jnp.maximum(logits, 0.0) + jnp.where(
                small < 1e-3, small - 0.5 * small * small, jnp.log(1.0 + small)
            )
            below = now * jnp.exp(down_rate * soft)
            upward[level] = jnp.exp(up_rate * soft)
            gone = jnp.sum(now - below, axis=1, keepdims=True)
            kept = jnp.where(lane == level, gone, kept)
            now = below
        return now, kept

    def upwards(part, carry):
        now, kept = carry
        for j in range(unroll):
            level = levels - 1 - (part * unroll + j)
            above = now * upward[level]
            gone = jnp.sum(now - above, axis=1, keepdims=True)
            kept = jnp.where(lane == level, kept + gone, kept)
            now = above
        return now, kept

    now, kept = lax.fori_loop(
        0, levels // unroll, downward,
        (flux_ref[...] * slant, jnp.zeros((columns, levels), F32)),
    )
    _, kept = lax.fori_loop(0, levels // unroll, upwards, (ALBEDO * now, kept))
    part_ref[...] = kept.reshape(specs, share, levels)

    backs = []
    for d in range(1, specs):
        other = lax.rem(spec + d, specs)
        backs.append(remote(
            part_ref.at[other], spec_in.at[d - 1], back_send.at[d - 1], back_recv.at[d - 1],
            (col, other),
        ))
    for one in backs:
        one.start()

    for one in corners:
        one.wait()

    def unpacked(value, count):
        return value.astype(F32).reshape(count, fields, levels)

    for x in range(halo):
        first[x, halo:halo + width_y] = unpacked(xl_ref[x], width_y)
        first[halo + width_x + x, halo:halo + width_y] = unpacked(xh_ref[x], width_y)

    @pl.loop(0, wide_x)
    def _(x):
        first[x, 0:halo] = unpacked(yl_ref[x], halo)
        first[x, halo + width_y:wide_y] = unpacked(yh_ref[x], halo)

    rate_x, rate_y = courant_x_ref[...], courant_y_ref[...]
    spread_x = 0.5 * rate_x * rate_x + DIFFUSION
    spread_y = 0.5 * rate_y * rate_y + DIFFUSION

    def wide(row):
        return jnp.broadcast_to(row, (fields, levels))[None]

    keep = wide(1.0 - 2.0 * spread_x - 2.0 * spread_y)
    from_east, from_west = wide(spread_x - 0.5 * rate_x), wide(spread_x + 0.5 * rate_x)
    from_north, from_south = wide(spread_y - 0.5 * rate_y), wide(spread_y + 0.5 * rate_y)
    buffers = (first, second)

    def advance(section):
        source, target = buffers[section % 2], buffers[(section + 1) % 2]
        low, high = section + 1, wide_y - section - 1
        last = section == SECTIONS - 1

        @pl.loop(section + 1, wide_x - section - 1)
        def _(x):
            value = (
                keep * source[x, low:high]
                + from_east * source[x + 1, low:high]
                + from_west * source[x - 1, low:high]
                + from_north * source[x, low + 1:high + 1]
                + from_south * source[x, low - 1:high - 1]
            )
            if last:
                state_ref[x - halo] = value
            else:
                target[x, low:high] = value

    for one in backs:
        one.wait()
    total = part_ref[spec]
    for d in range(1, specs):
        total = total + spec_in[d - 1]
    heat_ref[parity, k] = total
    gathers = []
    for d in range(1, half):
        gathers.append(remote(
            heat_ref.at[parity, k], heat_ref.at[parity, k], heat_send.at[d], heat_recv.at[d],
            (2 * lax.rem(k + d, half) + parity, spec),
        ))
    for one in gathers:
        one.start()
    for section in range(SECTIONS - 1):
        advance(section)
    for d in range(1, half):
        gathers[d - 1].wait_send()
        source = lax.rem(k + half - d, half)
        remote(
            heat_ref.at[parity, source], heat_ref.at[parity, source],
            heat_send.at[d], heat_recv.at[d],
            (2 * lax.rem(k + d, half) + parity, spec),
        ).wait_recv()
    last = remote(
        heat_ref.at[parity], heat_ref.at[parity], heat_send.at[0], heat_recv.at[0],
        (partner, spec),
    )
    last.start()
    advance(SECTIONS - 1)
    last.wait_send()
    remote(
        heat_ref.at[1 - parity], heat_ref.at[1 - parity], heat_send.at[0], heat_recv.at[0],
        (partner, spec),
    ).wait_recv()


def finish_kernel(share, width_y, place_ref, state_in_ref, index_ref, count_ref, heat_ref,
                  state_ref, grid_ref):
    cells, levels = grid_ref.shape
    width_x = cells // width_y
    col, spec = place_ref[0], place_ref[1]
    half = heat_ref.shape[1]
    grid = jnp.zeros((cells, levels), F32)
    for parity in range(2):
        ranks = rank_column([2 * k + parity for k in range(half)], share)
        cell = cell_column(ranks, count_ref[...], index_ref[0], spec, col)
        slots = cell.shape[0]
        lane = lax.broadcasted_iota(jnp.int32, (slots, cells), 1).astype(F32)
        choose = jnp.where(cell == lane, 1.0, 0.0).astype(BF16)
        rows = heat_ref[parity].reshape(slots, levels)
        upper = rows.astype(BF16)
        lower = (rows - upper.astype(F32)).astype(BF16)
        for piece in (upper, lower):
            grid = grid + lax.dot_general(
                choose, piece, (((0,), (0,)), ((), ())), preferred_element_type=F32
            )
    grid_ref[...] = grid

    @pl.loop(0, width_x)
    def _(x):
        start = pl.multiple_of(x * width_y, 8)
        state_ref[:, pl.ds(start, width_y), :] = pltpu.einshape("cfl->fcl", state_in_ref[x])
        state_ref[0, pl.ds(start, width_y), :] += grid_ref[pl.ds(start, width_y), :]


def on_device(
    air_state,
    courant_x,
    courant_y,
    cos_zenith,
    sun_index,
    sun_count,
    in_weight,
    in_bias,
    mid_weight,
    mid_bias,
    out_weight,
    out_bias,
    absorption,
    solar_flux,
):
    fields, width_x, width_y, levels = air_state.shape
    cells = width_x * width_y
    cols, specs = lax.axis_size("cols"), lax.axis_size("spec")
    half, quarter = cols // 2, cols // 4
    share = sun_index.shape[2] // 4
    halo = SECTIONS
    block = fields * share
    columns = specs * share
    points, hidden_size = out_weight.shape[1], out_weight.shape[2]
    air = air_state.reshape(fields, cells, levels)
    place = jnp.stack([lax.axis_index("cols"), lax.axis_index("spec")]).astype(jnp.int32)
    smem = pl.BlockSpec(memory_space=pltpu.SMEM)
    vmem = pl.BlockSpec(memory_space=pltpu.VMEM)
    dma = pltpu.SemaphoreType.DMA
    x_halo = pltpu.VMEM((halo, width_y * fields, levels), BF16)
    y_edge = pltpu.VMEM((width_x, halo * fields, levels), BF16)
    y_halo = pltpu.VMEM((width_x + 2 * halo, halo * fields, levels), BF16)
    wide = pltpu.VMEM((width_x + 2 * halo, width_y + 2 * halo, fields, levels), F32)

    state, heats = pl.pallas_call(
        functools.partial(main_kernel, cols, specs, share, halo, width_y),
        out_shape=(
            jax.ShapeDtypeStruct((width_x, width_y, fields, levels), F32),
            jax.ShapeDtypeStruct((2, half, share, levels), F32),
        ),
        in_specs=[vmem] * 10 + [pl.BlockSpec(memory_space=pl.ANY)] + [vmem] * 3,
        out_specs=(vmem, vmem),
        scratch_shapes=[
            pltpu.VMEM((2, quarter, block, levels), BF16),
            x_halo,
            x_halo,
            y_edge,
            y_edge,
            pltpu.VMEM((fields, half * share, levels), F32),
            pltpu.VMEM((specs, block, levels), BF16),
            x_halo,
            x_halo,
            y_halo,
            y_halo,
            pltpu.VMEM((2, quarter, block, levels), BF16),
            pltpu.VMEM((2, quarter, block, levels), BF16),
            pltpu.VMEM((quarter, block, levels), BF16),
            pltpu.VMEM((quarter, block, levels), BF16),
            pltpu.VMEM((quarter - 1, block, levels), BF16),
            pltpu.VMEM(out_weight.shape, BF16),
            pltpu.VMEM((specs * block, levels), F32),
            pltpu.VMEM((levels * columns, hidden_size), F32),
            pltpu.VMEM((levels, columns, points), F32),
            pltpu.VMEM((specs, share, levels), F32),
            pltpu.VMEM((specs - 1, share, levels), F32),
            wide,
            wide,
            dma,
            dma((10,)),
            dma((10,)),
            dma((quarter - 1,)),
            dma((quarter - 1,)),
            dma((specs - 1,)),
            dma((specs - 1,)),
            dma((specs - 1,)),
            dma((specs - 1,)),
            dma((half,)),
            dma((half,)),
        ],
        compiler_params=pltpu.CompilerParams(
            vmem_limit_bytes=VMEM_LIMIT, collective_id=0, has_side_effects=True
        ),
        name="main",
    )(air, cos_zenith, sun_index, sun_count, courant_x.reshape(1, -1), courant_y.reshape(1, -1),
      in_weight, in_bias.reshape(1, -1), mid_weight, mid_bias.reshape(1, -1), out_weight,
      out_bias.reshape(1, -1), absorption.reshape(1, -1), solar_flux.reshape(1, -1))

    state, grid = pl.pallas_call(
        functools.partial(finish_kernel, share, width_y),
        out_shape=(
            jax.ShapeDtypeStruct((fields, cells, levels), F32),
            jax.ShapeDtypeStruct((cells, levels), F32),
        ),
        in_specs=[smem] + [vmem] * 4,
        out_specs=(vmem, vmem),
        compiler_params=pltpu.CompilerParams(vmem_limit_bytes=VMEM_LIMIT),
        name="finish",
    )(place, state, sun_index, sun_count, heats)
    return (
        state.reshape(air_state.shape),
        grid.reshape(width_x, width_y, levels),
    )


def solution(mesh):
    placed = (
        P(None, "cols", "spec", None),
        P(),
        P(),
        P("cols", "spec"),
        P("cols", "spec", None),
        P(),
        P(),
        P(),
        P(),
        P(),
        P(None, "spec", None),
        P("spec"),
        P("spec"),
        P("spec"),
    )
    return jax.shard_map(
        on_device,
        mesh=mesh,
        in_specs=placed,
        out_specs=(P(None, "cols", "spec", None), P("cols", "spec", None)),
        check_vma=False,
    )
```

time: 183 us -> 50.6 us (0.28)
  Pallas kernels: 0 us -> 49.2 us
  local copies, waits for them, and re-layouts: 46.2 us -> 0 us
  starting transfers between devices: 35.5 us -> 0 us
  other arithmetic: 27.9 us -> 0.61 us
  waiting for transfers between devices: 24.5 us -> 0 us
  matrix products: 21.2 us -> 0 us
  between operations: 16.6 us -> 0.64 us
  blocking collectives: 9.62 us -> 0 us
    pallas_call x0 -> x2, Pallas kernels: none -> 49.2 us  [the longest x1 44.9 us: on_device(): pl.pallas_call(functools.partial(main_kernel, cols, specs, share, halo, w...]
    dot_general x9 -> x0, matrix products: 21.2 us -> none  [the longest x3 13.5 us: radiate_block(): jnp.einsum('lgh,lnh->lgn', out_weight, hidden_two, preferred_element_type...]
    ppermute x16 -> x0, starting transfers between devices: 20.5 us -> none  [the longest x8 16.9 us: padded_2(): lax.ppermute(head, axis, [((i + 1) % count, i) for i in range(count)])]
    all_to_all x3 -> x0, starting transfers between devices: 15 us -> none  [the longest x1 5.59 us: on_device(): lax.all_to_all(send_back, 'cols', split_axis=0, concat_axis=0, tiled=True)]
    unnamed x68 -> x0, local copies, waits for them, and re-layouts: 13 us -> none
    gather x13 -> x0, local copies, waits for them, and re-layouts: 12.8 us -> none  [the longest x5 3.49 us: on_device(): anchor = jnp.searchsorted(row_ends, slot_rank, side='right')]
    ppermute x16 -> x0, waiting for transfers between devices: 11.7 us -> none  [the longest x8 8.17 us: padded_2(): lax.ppermute(tail, axis, [(i, (i + 1) % count) for i in range(count)])]
    add x10 -> x0, other arithmetic: 10.7 us -> none  [the longest x4 8.75 us: section_update(): centre - 0.5 * courant_x * (eastern - western)]
  transfers between devices with their start and end apart: 20 -> 0, of which waited for: 8 -> 0; matrix products, arithmetic and copies ran while one was open for 40% -> 0% of each run, Pallas kernels for 0% -> 0%
where the time goes in v2:
time: 50.6 us; the launch traced here: 50.4 us
  Pallas kernels  49.2 us (97%)
  between operations  0.64 us (1%)
  other arithmetic  0.61 us (1%)
    pallas_call x1, Pallas kernels, on_device(): pl.pallas_call(functools.partial(main_kernel, cols, specs, share, halo, w...  44.9 us
    pallas_call x1, Pallas kernels, on_device(): pl.pallas_call(functools.partial(finish_kernel, share, width_y), out_shap...  4.23 us

profile of v2, /device:TPU:0, one launch (start us, length us, event | category | flops | bytes accessed | tf_op | source)
XLA Modules:
  0.0 50.4 jit_solution(9204326399710221346)
XLA Ops:
  0.6 0.6 %pad_add_fusion.place_ref = s32[2]{0:T(128)} fusion(s32[1]{0:T(128)} %bitcast.1, s32[1]{0:T(128)} %bitcast), kind=kLoop, calls=%fused_computation | loop fusion | flops 2 | bytes 16 | tf_op jit(solution)/shard_map/stack | solution.py:425
  1.2 44.9 %main.1 = (f32[16,32,8,128]{3,2,1,0:T(8,128)}, f32[2,8,24,128]{3,2,1,0:T(8,128)}) custom-call(f32[8,512,128]{2,1,0:T(8,128)} %bitcast.12, f32[16,32]{1,0:T(8,128)} %cos_ref.1, s32[1,1,96]{2,1,0:T(1,128)} %index_ref.3, s32[2,16]{1,0:T(2,128)} %count_ref.3, f32[1,128]{1,0:T(1,128)} %bitcast.13, f32[1,128]{1,0:T(1,128)} %bitcast.14, ...), custom_call_target="tpu_custom_call" | custom-call | tf_op jit(solution)/shard_map/main/pallas_call | solution.py:434
  46.2 4.2 %finish.1 = (f32[8,512,128]{2,1,0:T(8,128)}, f32[512,128]{1,0:T(8,128)}) custom-call(s32[2]{0:T(128)} %pad_add_fusion.place_ref, f32[16,32,8,128]{3,2,1,0:T(8,128)} %get-tuple-element.6.state_in_ref, s32[1,1,96]{2,1,0:T(1,128)} %index_ref.3, s32[2,16]{1,0:T(2,128)} %count_ref.3, f32[2,8,24,128]{3,2,1,0:T(8,128)} %get-tuple-element.7.heat_ref), custom_call_target="tpu_custom_call" | custom-call | tf_op jit(solution)/shard_map/finish/pallas_call | solution.py:487

commit v3 on v2

--- a/solution.py
+++ b/solution.py
@@ -8,6 +8,8 @@
 from jax.sharding import PartitionSpec as P
 
 SECTIONS = 4
+CHUNKS = 2
+LOG2_E = 1.4426950408889634
 DIFFUSION = 0.05
 ALBEDO = 0.3
 DIFFUSIVITY = 1.66
@@ -62,6 +64,8 @@
     wide_x, wide_y = width_x + 2 * halo, width_y + 2 * halo
     columns = specs * share
     block = fields * share
+    group_fields = fields // CHUNKS
+    piece_rows = group_fields * share
     col, spec = lax.axis_index("cols"), lax.axis_index("spec")
     half, quarter = cols // 2, cols // 4
     parity, k = lax.rem(col, 2), lax.div(col, 2)
@@ -84,7 +88,7 @@
 
     counts, index_row = count_ref[...], index_ref[0]
 
-    def pack(which):
+    def choice(which):
         ranks = rank_column(
             [4 * c + 2 * b + which for b in range(2) for c in range(quarter)], share
         )
@@ -92,34 +96,54 @@
         slots = cell.shape[0]
         lane = lax.broadcasted_iota(jnp.int32, (slots, cells), 1).astype(F32)
         choose = jnp.where(cell == lane, 1.0, 0.0).astype(BF16)
-        for i in range(inputs):
-            picked[i] = jnp.dot(choose, air_ref[i].astype(BF16), preferred_element_type=F32)
-        cell_x = jnp.floor((cell + 0.5) * (1.0 / width_y))
-        cell_y = cell - cell_x * width_y
-        lane_x = lax.broadcasted_iota(jnp.int32, (slots, width_x), 1).astype(F32)
-        lane_y = lax.broadcasted_iota(jnp.int32, (slots, width_y), 1).astype(F32)
-        by_x = jnp.dot(
-            jnp.where(cell_x == lane_x, 1.0, 0.0).astype(BF16),
-            cos_ref[...].astype(BF16),
-            preferred_element_type=F32,
-        )
-        slant = jnp.sum(jnp.where(cell_y == lane_y, by_x, 0.0), axis=1, keepdims=True)
-        picked[inputs] = jnp.broadcast_to(slant, (slots, levels))
+        return cell, choose
+
+    def pack(chosen, chunk):
+        cell, choose = chosen
+        slots = cell.shape[0]
+        for at in range(group_fields):
+            i = chunk * group_fields + at
+            if i < inputs:
+                picked[at] = jnp.dot(
+                    choose, air_ref[i].astype(BF16), preferred_element_type=F32
+                )
+                continue
+            cell_x = jnp.floor((cell + 0.5) * (1.0 / width_y))
+            cell_y = cell - cell_x * width_y
+            lane_x = lax.broadcasted_iota(jnp.int32, (slots, width_x), 1).astype(F32)
+            lane_y = lax.broadcasted_iota(jnp.int32, (slots, width_y), 1).astype(F32)
+            by_x = jnp.dot(
+                jnp.where(cell_x == lane_x, 1.0, 0.0).astype(BF16),
+                cos_ref[...].astype(BF16),
+                preferred_element_type=F32,
+            )
+            slant = jnp.sum(jnp.where(cell_y == lane_y, by_x, 0.0), axis=1, keepdims=True)
+            picked[at] = jnp.broadcast_to(slant, (slots, levels))
         blocks = []
         for at in range(half):
             piece = picked[:, at * share:(at + 1) * share, :]
-            blocks.append(piece.reshape(block, levels).astype(BF16)[None])
-        return jnp.concatenate(blocks, axis=0).reshape(2, quarter, block, levels)
-
-    send_ref[...] = pack(1 - parity)
-    pl.semaphore_wait(barrier, len(peers))
-    pair = copy(send_ref, pair_in, 0, (partner, spec))
-    pair.start()
-    merged[...] = pack(parity)
-    pair.wait()
-    merged[...] = merged[...] + pair_in[...]
-    over = copy(merged.at[1 - bit], next_in, 9, (across, spec))
-    over.start()
+            blocks.append(piece.reshape(piece_rows, levels).astype(BF16)[None])
+        return jnp.concatenate(blocks, axis=0).reshape(2, quarter, piece_rows, levels)
+
+    chosen = choice(1 - parity)
+    pairs = [
+        copy(send_ref.at[c], pair_in.at[c], 10 + c, (partner, spec)) for c in range(CHUNKS)
+    ]
+    overs = [
+        copy(merged.at[c, 1 - bit], next_in.at[c], 10 + CHUNKS + c, (across, spec))
+        for c in range(CHUNKS)
+    ]
+    for c in range(CHUNKS):
+        send_ref[c] = pack(chosen, c)
+        if c == 0:
+            pl.semaphore_wait(barrier, len(peers))
+        pairs[c].start()
+    chosen = choice(parity)
+    for c in range(CHUNKS):
+        merged[c] = pack(chosen, c)
+        pairs[c].wait()
+        merged[c] = merged[c] + pair_in[c]
+        overs[c].start()
 
     def cells_of(start, count):
         piece = air_ref[:, pl.ds(start, count), :]
@@ -128,17 +152,19 @@
     for x in range(halo):
         xlow_ref[x] = cells_of(x * width_y, width_y)
         xhigh_ref[x] = cells_of((width_x - halo + x) * width_y, width_y)
-    over.wait()
-    narrowed[...] = merged[bit] + next_in[...]
     groups = []
-    for d in range(1, quarter):
-        other = lax.rem(kk + d, quarter)
-        groups.append(remote(
-            narrowed.at[other], group_in.at[d - 1], group_send.at[d - 1], group_recv.at[d - 1],
-            (4 * other + 2 * bit + parity, spec),
-        ))
-    for one in groups:
-        one.start()
+    for c in range(CHUNKS):
+        overs[c].wait()
+        narrowed[c] = merged[c, bit] + next_in[c]
+        for d in range(1, quarter):
+            other = lax.rem(kk + d, quarter)
+            number = c * (quarter - 1) + d - 1
+            groups.append(remote(
+                narrowed.at[c, other], group_in.at[number],
+                group_send.at[number], group_recv.at[number],
+                (4 * other + 2 * bit + parity, spec),
+            ))
+            groups[-1].start()
 
     @pl.loop(0, width_x)
     def _(x):
@@ -147,20 +173,22 @@
         ylow_ref[x] = low[:halo * fields]
         yhigh_ref[x] = high[(8 - halo) * fields:]
 
-    for one in groups:
-        one.wait()
-    total = narrowed[kk]
-    for d in range(1, quarter):
-        total = total + group_in[d - 1]
-    feat_ref[spec] = total
     spreads = []
-    for d in range(1, specs):
-        spreads.append(remote(
-            feat_ref.at[spec], feat_ref.at[spec], spec_send.at[d - 1], spec_recv.at[d - 1],
-            (col, lax.rem(spec + d, specs)),
-        ))
-    for one in spreads:
-        one.start()
+    for c in range(CHUNKS):
+        total = narrowed[c, kk]
+        for d in range(1, quarter):
+            number = c * (quarter - 1) + d - 1
+            groups[number].wait()
+            total = total + group_in[number]
+        feat_ref[spec, c] = total
+        for d in range(1, specs):
+            number = c * (specs - 1) + d - 1
+            spreads.append(remote(
+                feat_ref.at[spec, c], feat_ref.at[spec, c],
+                spec_send.at[number], spec_recv.at[number],
+                (col, lax.rem(spec + d, specs)),
+            ))
+            spreads[-1].start()
     rows = ylow_ref.shape[1]
     row_end = xlow_ref.shape[1]
     sides = [
@@ -177,16 +205,21 @@
         piece = air_ref[:, pl.ds(pl.multiple_of(x * width_y, 8), width_y), :]
         first[x + halo, halo:halo + width_y] = pltpu.einshape("fcl->cfl", piece)
 
-    for d in range(1, specs):
-        spreads[d - 1].wait_send()
-        source = lax.rem(spec + specs - d, specs)
-        remote(
-            feat_ref.at[source], feat_ref.at[source], spec_send.at[d - 1], spec_recv.at[d - 1],
-            (col, lax.rem(spec + d, specs)),
-        ).wait_recv()
+    for c in range(CHUNKS):
+        for d in range(1, specs):
+            number = c * (specs - 1) + d - 1
+            spreads[number].wait_send()
+            source = lax.rem(spec + specs - d, specs)
+            remote(
+                feat_ref.at[source, c], feat_ref.at[source, c],
+                spec_send.at[number], spec_recv.at[number],
+                (col, lax.rem(spec + d, specs)),
+            ).wait_recv()
 
     for s in range(specs):
-        feats[s * block:(s + 1) * block, :] = feat_ref[s].astype(F32)
+        for c in range(CHUNKS):
+            start = s * block + c * piece_rows
+            feats[start:start + piece_rows, :] = feat_ref[s, c].astype(F32)
     slant = jnp.concatenate(
         [feats[s * block + inputs * share:(s + 1) * block, :] for s in range(specs)], axis=0
     )[:, :1]
@@ -231,8 +264,8 @@
     fetch.wait()
 
     absorption = absorption_ref[...]
-    down_rate = -(absorption / slant)
-    up_rate = -DIFFUSIVITY * absorption
+    down_rate = -LOG2_E * (absorption / slant)
+    up_rate = -DIFFUSIVITY * LOG2_E * absorption
     out_bias = out_bias_ref[...]
     lane = lax.broadcasted_iota(jnp.int32, (columns, levels), 1)
     unroll = 16
@@ -250,8 +283,8 @@
             soft = jnp.maximum(logits, 0.0) + jnp.where(
                 small < 1e-3, small - 0.5 * small * small, jnp.log(1.0 + small)
             )
-            below = now * jnp.exp(down_rate * soft)
-            upward[level] = jnp.exp(up_rate * soft)
+            below = now * jnp.exp2(down_rate * soft)
+            upward[level] = jnp.exp2(up_rate * soft)
             gone = jnp.sum(now - below, axis=1, keepdims=True)
             kept = jnp.where(lane == level, gone, kept)
             now = below
@@ -367,18 +400,19 @@
     ).wait_recv()
 
 
-def finish_kernel(share, width_y, place_ref, state_in_ref, index_ref, count_ref, heat_ref,
+def finish_kernel(share, width_y, state_in_ref, index_ref, count_ref, heat_ref,
                   state_ref, grid_ref):
     cells, levels = grid_ref.shape
     width_x = cells // width_y
-    col, spec = place_ref[0], place_ref[1]
+    col, spec = lax.axis_index("cols"), lax.axis_index("spec")
     half = heat_ref.shape[1]
+    before = pl.program_id(0) * cells
     grid = jnp.zeros((cells, levels), F32)
     for parity in range(2):
         ranks = rank_column([2 * k + parity for k in range(half)], share)
         cell = cell_column(ranks, count_ref[...], index_ref[0], spec, col)
         slots = cell.shape[0]
-        lane = lax.broadcasted_iota(jnp.int32, (slots, cells), 1).astype(F32)
+        lane = (lax.broadcasted_iota(jnp.int32, (slots, cells), 1) + before).astype(F32)
         choose = jnp.where(cell == lane, 1.0, 0.0).astype(BF16)
         rows = heat_ref[parity].reshape(slots, levels)
         upper = rows.astype(BF16)
@@ -388,12 +422,11 @@
                 choose, piece, (((0,), (0,)), ((), ())), preferred_element_type=F32
             )
     grid_ref[...] = grid
-
-    @pl.loop(0, width_x)
-    def _(x):
-        start = pl.multiple_of(x * width_y, 8)
-        state_ref[:, pl.ds(start, width_y), :] = pltpu.einshape("cfl->fcl", state_in_ref[x])
-        state_ref[0, pl.ds(start, width_y), :] += grid_ref[pl.ds(start, width_y), :]
+    for x in range(width_x):
+        start = x * width_y
+        block = pltpu.einshape("cfl->fcl", state_in_ref[x])
+        state_ref[:, start:start + width_y, :] = block
+        state_ref[0, start:start + width_y, :] = block[0] + grid[start:start + width_y]
 
 
 def on_device(
@@ -419,11 +452,10 @@
     share = sun_index.shape[2] // 4
     halo = SECTIONS
     block = fields * share
+    piece = block // CHUNKS
     columns = specs * share
     points, hidden_size = out_weight.shape[1], out_weight.shape[2]
     air = air_state.reshape(fields, cells, levels)
-    place = jnp.stack([lax.axis_index("cols"), lax.axis_index("spec")]).astype(jnp.int32)
-    smem = pl.BlockSpec(memory_space=pltpu.SMEM)
     vmem = pl.BlockSpec(memory_space=pltpu.VMEM)
     dma = pltpu.SemaphoreType.DMA
     x_halo = pltpu.VMEM((halo, width_y * fields, levels), BF16)
@@ -440,22 +472,22 @@
         in_specs=[vmem] * 10 + [pl.BlockSpec(memory_space=pl.ANY)] + [vmem] * 3,
         out_specs=(vmem, vmem),
         scratch_shapes=[
-            pltpu.VMEM((2, quarter, block, levels), BF16),
+            pltpu.VMEM((CHUNKS, 2, quarter, piece, levels), BF16),
             x_halo,
             x_halo,
             y_edge,
             y_edge,
-            pltpu.VMEM((fields, half * share, levels), F32),
-            pltpu.VMEM((specs, block, levels), BF16),
+            pltpu.VMEM((fields // CHUNKS, half * share, levels), F32),
+            pltpu.VMEM((specs, CHUNKS, piece, levels), BF16),
             x_halo,
             x_halo,
             y_halo,
             y_halo,
-            pltpu.VMEM((2, quarter, block, levels), BF16),
-            pltpu.VMEM((2, quarter, block, levels), BF16),
-            pltpu.VMEM((quarter, block, levels), BF16),
-            pltpu.VMEM((quarter, block, levels), BF16),
-            pltpu.VMEM((quarter - 1, block, levels), BF16),
+            pltpu.VMEM((CHUNKS, 2, quarter, piece, levels), BF16),
+            pltpu.VMEM((CHUNKS, 2, quarter, piece, levels), BF16),
+            pltpu.VMEM((CHUNKS, quarter, piece, levels), BF16),
+            pltpu.VMEM((CHUNKS, quarter, piece, levels), BF16),
+            pltpu.VMEM((CHUNKS * (quarter - 1), piece, levels), BF16),
             pltpu.VMEM(out_weight.shape, BF16),
             pltpu.VMEM((specs * block, levels), F32),
             pltpu.VMEM((levels * columns, hidden_size), F32),
@@ -465,12 +497,12 @@
             wide,
             wide,
             dma,
-            dma((10,)),
-            dma((10,)),
-            dma((quarter - 1,)),
-            dma((quarter - 1,)),
-            dma((specs - 1,)),
-            dma((specs - 1,)),
+            dma((10 + 2 * CHUNKS,)),
+            dma((10 + 2 * CHUNKS,)),
+            dma((CHUNKS * (quarter - 1),)),
+            dma((CHUNKS * (quarter - 1),)),
+            dma((CHUNKS * (specs - 1),)),
+            dma((CHUNKS * (specs - 1),)),
             dma((specs - 1,)),
             dma((specs - 1,)),
             dma((half,)),
@@ -484,17 +516,27 @@
       in_weight, in_bias.reshape(1, -1), mid_weight, mid_bias.reshape(1, -1), out_weight,
       out_bias.reshape(1, -1), absorption.reshape(1, -1), solar_flux.reshape(1, -1))
 
+    steps = 4
     state, grid = pl.pallas_call(
         functools.partial(finish_kernel, share, width_y),
         out_shape=(
             jax.ShapeDtypeStruct((fields, cells, levels), F32),
             jax.ShapeDtypeStruct((cells, levels), F32),
         ),
-        in_specs=[smem] + [vmem] * 4,
-        out_specs=(vmem, vmem),
+        grid=(steps,),
+        in_specs=[
+            pl.BlockSpec((width_x // steps, width_y, fields, levels), lambda i: (i, 0, 0, 0)),
+            pl.BlockSpec(sun_index.shape, lambda i: (0, 0, 0)),
+            pl.BlockSpec(sun_count.shape, lambda i: (0, 0)),
+            pl.BlockSpec(heats.shape, lambda i: (0, 0, 0, 0)),
+        ],
+        out_specs=(
+            pl.BlockSpec((fields, cells // steps, levels), lambda i: (0, i, 0)),
+            pl.BlockSpec((cells // steps, levels), lambda i: (i, 0)),
+        ),
         compiler_params=pltpu.CompilerParams(vmem_limit_bytes=VMEM_LIMIT),
         name="finish",
-    )(place, state, sun_index, sun_count, heats)
+    )(state, sun_index, sun_count, heats)
     return (
         state.reshape(air_state.shape),
         grid.reshape(width_x, width_y, levels),

time: 50.6 us -> 48.9 us (0.966)
  Pallas kernels: 49.2 us -> 48 us
  other arithmetic: 0.61 us -> 0 us
    pallas_call x1, Pallas kernels: 44.9 us -> 42.9 us  [on_device(): pl.pallas_call(functools.partial(main_kernel, cols, specs, share, halo, w...]
    pallas_call x1, Pallas kernels: 4.23 us -> 5.09 us  [on_device(): pl.pallas_call(functools.partial(finish_kernel, share, width_y), out_shap...]
    another operation x1 -> x0, other arithmetic: 0.61 us -> none  [on_device(): jnp.stack([lax.axis_index('cols'), lax.axis_index('spec')])]
where the time goes in v3:
time: 48.9 us; the launch traced here: 48.7 us
  Pallas kernels  48 us (98%)
  between operations  0.64 us (1%)
    pallas_call x1, Pallas kernels, on_device(): pl.pallas_call(functools.partial(main_kernel, cols, specs, share, halo, w...  42.9 us
    pallas_call x1, Pallas kernels, on_device(): pl.pallas_call(functools.partial(finish_kernel, share, width_y), out_shap...  5.09 us

profile of v3, /device:TPU:0, one launch (start us, length us, event | category | flops | bytes accessed | tf_op | source)
XLA Modules:
  0.0 48.7 jit_solution(2558657782583326775)
XLA Ops:
  0.6 42.9 %main.1 = (f32[16,32,8,128]{3,2,1,0:T(8,128)}, f32[2,8,24,128]{3,2,1,0:T(8,128)}) custom-call(f32[8,512,128]{2,1,0:T(8,128)} %bitcast.10, f32[16,32]{1,0:T(8,128)} %cos_ref.1, s32[1,1,96]{2,1,0:T(1,128)} %index_ref.3, s32[2,16]{1,0:T(2,128)} %count_ref.3, f32[1,128]{1,0:T(1,128)} %bitcast.11, f32[1,128]{1,0:T(1,128)} %bitcast.12, ...), custom_call_target="tpu_custom_call" | custom-call | tf_op jit(solution)/shard_map/main/pallas_call | solution.py:466
  43.6 5.1 %finish.1 = (f32[8,512,128]{2,1,0:T(8,128)}, f32[512,128]{1,0:T(8,128)}) custom-call(f32[16,32,8,128]{3,2,1,0:T(8,128)} %get-tuple-element.6.state_in_ref, s32[1,1,96]{2,1,0:T(1,128)} %index_ref.3, s32[2,16]{1,0:T(2,128)} %count_ref.3, f32[2,8,24,128]{3,2,1,0:T(8,128)} %get-tuple-element.7.heat_ref), custom_call_target="tpu_custom_call" | custom-call | tf_op jit(solution)/shard_map/finish/pallas_call | solution.py:520

commit v4 on v3

--- a/solution.py
+++ b/solution.py
@@ -401,32 +401,35 @@
 
 
 def finish_kernel(share, width_y, state_in_ref, index_ref, count_ref, heat_ref,
-                  state_ref, grid_ref):
-    cells, levels = grid_ref.shape
-    width_x = cells // width_y
-    col, spec = lax.axis_index("cols"), lax.axis_index("spec")
-    half = heat_ref.shape[1]
-    before = pl.program_id(0) * cells
-    grid = jnp.zeros((cells, levels), F32)
-    for parity in range(2):
-        ranks = rank_column([2 * k + parity for k in range(half)], share)
+                  state_ref, grid_ref, whole_ref):
+    rows, levels = grid_ref.shape
+    cells = whole_ref.shape[0]
+    width_x = rows // width_y
+    step = pl.program_id(0)
+
+    @pl.when(step == 0)
+    def _():
+        col, spec = lax.axis_index("cols"), lax.axis_index("spec")
+        half = heat_ref.shape[1]
+        ranks = rank_column([2 * k + parity for parity in range(2) for k in range(half)], share)
         cell = cell_column(ranks, count_ref[...], index_ref[0], spec, col)
         slots = cell.shape[0]
-        lane = (lax.broadcasted_iota(jnp.int32, (slots, cells), 1) + before).astype(F32)
-        choose = jnp.where(cell == lane, 1.0, 0.0).astype(BF16)
-        rows = heat_ref[parity].reshape(slots, levels)
-        upper = rows.astype(BF16)
-        lower = (rows - upper.astype(F32)).astype(BF16)
-        for piece in (upper, lower):
-            grid = grid + lax.dot_general(
-                choose, piece, (((0,), (0,)), ((), ())), preferred_element_type=F32
-            )
-    grid_ref[...] = grid
+        across = jnp.transpose(jnp.broadcast_to(cell, (slots, 128)))[:1]
+        owner = lax.broadcasted_iota(jnp.int32, (cells, slots), 0).astype(F32)
+        choose = jnp.where(across == owner, 1.0, 0.0).astype(BF16)
+        heats = heat_ref[...].reshape(slots, levels)
+        upper = heats.astype(BF16)
+        lower = (heats - upper.astype(F32)).astype(BF16)
+        whole_ref[...] = jnp.dot(choose, upper, preferred_element_type=F32) + jnp.dot(
+            choose, lower, preferred_element_type=F32
+        )
+
+    grid_ref[...] = whole_ref[pl.ds(pl.multiple_of(step * rows, 8), rows), :]
     for x in range(width_x):
         start = x * width_y
         block = pltpu.einshape("cfl->fcl", state_in_ref[x])
         state_ref[:, start:start + width_y, :] = block
-        state_ref[0, start:start + width_y, :] = block[0] + grid[start:start + width_y]
+        state_ref[0, start:start + width_y, :] = block[0] + grid_ref[start:start + width_y, :]
 
 
 def on_device(
@@ -534,6 +537,7 @@
             pl.BlockSpec((fields, cells // steps, levels), lambda i: (0, i, 0)),
             pl.BlockSpec((cells // steps, levels), lambda i: (i, 0)),
         ),
+        scratch_shapes=[pltpu.VMEM((cells, levels), F32)],
         compiler_params=pltpu.CompilerParams(vmem_limit_bytes=VMEM_LIMIT),
         name="finish",
     )(state, sun_index, sun_count, heats)

time: 48.9 us -> 48.5 us (level)
  no operation moved by 1% of the time
where the time goes in v4:
time: 48.5 us; the launch traced here: 48.3 us
  Pallas kernels  47.6 us (98%)
  between operations  0.64 us (1%)
    pallas_call x1, Pallas kernels, on_device(): pl.pallas_call(functools.partial(main_kernel, cols, specs, share, halo, w...  42.9 us
    pallas_call x1, Pallas kernels, on_device(): pl.pallas_call(functools.partial(finish_kernel, share, width_y), out_shap...  4.71 us

profile of v4, /device:TPU:0, one launch (start us, length us, event | category | flops | bytes accessed | tf_op | source)
XLA Modules:
  0.0 48.3 jit_solution(3735326419462712178)
XLA Ops:
  0.6 42.9 %main.1 = (f32[16,32,8,128]{3,2,1,0:T(8,128)}, f32[2,8,24,128]{3,2,1,0:T(8,128)}) custom-call(f32[8,512,128]{2,1,0:T(8,128)} %bitcast.10, f32[16,32]{1,0:T(8,128)} %cos_ref.1, s32[1,1,96]{2,1,0:T(1,128)} %index_ref.3, s32[2,16]{1,0:T(2,128)} %count_ref.3, f32[1,128]{1,0:T(1,128)} %bitcast.11, f32[1,128]{1,0:T(1,128)} %bitcast.12, ...), custom_call_target="tpu_custom_call" | custom-call | tf_op jit(solution)/shard_map/main/pallas_call | solution.py:469
  43.6 4.7 %finish.1 = (f32[8,512,128]{2,1,0:T(8,128)}, f32[512,128]{1,0:T(8,128)}) custom-call(f32[16,32,8,128]{3,2,1,0:T(8,128)} %get-tuple-element.6.state_in_ref, s32[1,1,96]{2,1,0:T(1,128)} %index_ref.3, s32[2,16]{1,0:T(2,128)} %count_ref.3, f32[2,8,24,128]{3,2,1,0:T(8,128)} %get-tuple-element.7.heat_ref), custom_call_target="tpu_custom_call" | custom-call | tf_op jit(solution)/shard_map/finish/pallas_call | solution.py:523
